TPU v7x, 512 devices: a whole 4x4x16 slice. The times are simulated.
512 devices in a mesh: dp: 8 (over z_lo), tm: 4 (over z_hi, core), space: 16 (over y, x).
Axes of the slice: x: 4, y: 4, z: 16 (z_hi: 2, z_lo: 8; z = z_hi * 8 + z_lo), core: 2. Of those that a mesh axis runs over, the one named last changes fastest.
Arguments:
- patches: bfloat16 [8, 8, 1024, 1152], P('dp', 'tm', 'space'), may hold values from -4 to 4
- query_s: bfloat16 [8, 8, 1024, 1152], P('dp', 'tm', 'space'), may hold values from -8 to 8
- key_s: bfloat16 [8, 8, 1024, 1152], P('dp', 'tm', 'space'), may hold values from -8 to 8
- value_s: bfloat16 [8, 8, 1024, 1152], P('dp', 'tm', 'space'), may hold values from -6 to 6
- query_t: bfloat16 [8, 8, 1024, 1152], P('dp', 'tm', 'space'), may hold values from -8 to 8
- key_t: bfloat16 [8, 8, 1024, 1152], P('dp', 'tm', 'space'), may hold values from -8 to 8
- value_t: bfloat16 [8, 8, 1024, 1152], P('dp', 'tm', 'space'), may hold values from -6 to 6
- adapters_a: bfloat16 [4, 1152, 16], replicated, may hold values from -0.1875 to 0.1875
- adapters_b: bfloat16 [4, 16, 1152], replicated, may hold values from -1.5 to 1.5
- cotangent: bfloat16 [8, 8, 1024, 1152], P('dp', 'tm', 'space'), may hold values from -6 to 6
Outputs:
- mixed: bfloat16 [8, 8, 1024, 1152], P('dp', 'tm', 'space')
- grads_a: float32 [4, 1152, 16], replicated
- grads_b: float32 [4, 16, 1152], replicated
All inputs are finite; a program needn't handle non-finite values.
Results may differ from a plain program's by a relative error of at most 0.018.
The roundings to bfloat16 on the way count: a program that leaves them out, or rounds other values in their place, can miss the bound.
Values may be sent and summed in bfloat16 or wider, within the bound.
A program may use at most 64 MiB of HBM per device.

v0:
```python
import jax
import jax.numpy as jnp
from jax import lax
from jax.sharding import PartitionSpec as P

HEAD_DIM = 72


def softmax_probs(query, keys):
    length, columns = query.shape
    heads_here = columns // HEAD_DIM
    heads_q = query.reshape(length, heads_here, HEAD_DIM)
    heads_k = keys.reshape(keys.shape[0], heads_here, HEAD_DIM)
    scores = jnp.einsum(
        "qhd,khd->hqk", heads_q, heads_k, preferred_element_type=jnp.float32
    ) * HEAD_DIM ** (-0.5)
    peak = jnp.max(scores, axis=-1, keepdims=True)
    weights = jnp.exp(scores - peak)
    return weights / jnp.sum(weights, axis=-1, keepdims=True)


def attend_forward(query, keys, values):
    length, columns = query.shape
    heads_here = columns // HEAD_DIM
    probs_low = softmax_probs(query, keys).astype(jnp.bfloat16)
    heads_v = values.reshape(values.shape[0], heads_here, HEAD_DIM)
    output = jnp.einsum("hqk,khd->qhd", probs_low, heads_v, preferred_element_type=jnp.float32)
    return output.reshape(length, columns).astype(jnp.bfloat16)


def attend_backward(query, keys, values, grad):
    length, columns = query.shape
    count = keys.shape[0]
    heads_here = columns // HEAD_DIM
    probs = softmax_probs(query, keys)
    probs_low = probs.astype(jnp.bfloat16)
    heads_g = grad.reshape(length, heads_here, HEAD_DIM)
    heads_v = values.reshape(count, heads_here, HEAD_DIM)
    heads_k = keys.reshape(count, heads_here, HEAD_DIM)
    dvals = jnp.einsum("hqk,qhd->khd", probs_low, heads_g, preferred_element_type=jnp.float32)
    dprob = jnp.einsum("qhd,khd->hqk", heads_g, heads_v, preferred_element_type=jnp.float32)
    inner = jnp.sum(probs * dprob, axis=-1, keepdims=True)
    dscore = (probs * (dprob - inner) * HEAD_DIM ** (-0.5)).astype(jnp.bfloat16)
    dquery = jnp.einsum("hqk,khd->qhd", dscore, heads_k, preferred_element_type=jnp.float32)
    return (
        dquery.reshape(length, columns).astype(jnp.bfloat16),
        dvals.reshape(count, columns).astype(jnp.bfloat16),
    )


def per_device(
    patches, query_s, key_s, value_s, query_t, key_t, value_t, adapters_a, adapters_b, cotangent
):
    inputs = patches[0]
    frames_dev, patch_dev, width = inputs.shape

    def encode(source, index):
        return jnp.dot(
            source.reshape(-1, width), adapters_a[index], preferred_element_type=jnp.float32
        ).astype(jnp.bfloat16)

    def adapted(base, codes, index):
        lifted = base.reshape(-1, width).astype(jnp.float32) + jnp.dot(
            codes, adapters_b[index], preferred_element_type=jnp.float32
        )
        return lifted.astype(jnp.bfloat16).reshape(frames_dev, patch_dev, width)

    def token_grads(codes, dproj, index):
        flat_dproj = dproj.reshape(-1, width)
        grad_b = jnp.dot(codes.T, flat_dproj, preferred_element_type=jnp.float32)
        dcodes = jnp.dot(
            flat_dproj, adapters_b[index].T, preferred_element_type=jnp.float32
        ).astype(jnp.bfloat16)
        return (grad_b, dcodes)

    def down_grad(source, dcodes):
        return jnp.dot(source.reshape(-1, width).T, dcodes, preferred_element_type=jnp.float32)

    codes_sq = encode(inputs, 0)
    codes_sv = encode(inputs, 1)
    q_s = adapted(query_s[0], codes_sq, 0)
    v_s = adapted(value_s[0], codes_sv, 1)
    space_q, space_k, space_v = (
        lax.all_to_all(q_s, "space", split_axis=2, concat_axis=1, tiled=True),
        lax.all_to_all(key_s[0], "space", split_axis=2, concat_axis=1, tiled=True),
        lax.all_to_all(v_s, "space", split_axis=2, concat_axis=1, tiled=True),
    )
    out_s = lax.map(
        lambda trio: attend_forward(trio[0], trio[1], trio[2]), (space_q, space_k, space_v)
    )
    back_s = lax.all_to_all(out_s, "space", split_axis=1, concat_axis=2, tiled=True)
    hidden = (inputs.astype(jnp.float32) + back_s.astype(jnp.float32)).astype(jnp.bfloat16)
    codes_tq = encode(hidden, 2)
    codes_tv = encode(hidden, 3)
    q_t = adapted(query_t[0], codes_tq, 2)
    v_t = adapted(value_t[0], codes_tv, 3)
    time_q, time_k, time_v = (
        lax.all_to_all(q_t, "tm", split_axis=2, concat_axis=0, tiled=True),
        lax.all_to_all(key_t[0], "tm", split_axis=2, concat_axis=0, tiled=True),
        lax.all_to_all(v_t, "tm", split_axis=2, concat_axis=0, tiled=True),
    )
    out_t = jax.vmap(attend_forward, in_axes=1, out_axes=1)(time_q, time_k, time_v)
    back_t = lax.all_to_all(out_t, "tm", split_axis=0, concat_axis=2, tiled=True)
    mixed = (hidden.astype(jnp.float32) + back_t.astype(jnp.float32)).astype(jnp.bfloat16)
    grad = cotangent[0]
    grad_time = lax.all_to_all(grad, "tm", split_axis=2, concat_axis=0, tiled=True)
    dq_time, dv_time = jax.vmap(attend_backward, in_axes=1, out_axes=1)(
        time_q, time_k, time_v, grad_time
    )
    dq_t, dv_t = (
        lax.all_to_all(dq_time, "tm", split_axis=0, concat_axis=2, tiled=True),
        lax.all_to_all(dv_time, "tm", split_axis=0, concat_axis=2, tiled=True),
    )
    gb_tq, dcodes_tq = token_grads(codes_tq, dq_t, 2)
    gb_tv, dcodes_tv = token_grads(codes_tv, dv_t, 3)
    ga_tq = down_grad(hidden, dcodes_tq)
    ga_tv = down_grad(hidden, dcodes_tv)
    factor = (
        frames_dev * patch_dev * lax.axis_size("dp") * lax.axis_size("tm") * lax.axis_size("space")
    ) ** (-0.5)
    dhidden = grad.reshape(-1, width).astype(jnp.float32)
    dhidden = dhidden + jnp.dot(dcodes_tq, adapters_a[2].T, preferred_element_type=jnp.float32)
    dhidden = dhidden + jnp.dot(dcodes_tv, adapters_a[3].T, preferred_element_type=jnp.float32)
    dhidden = dhidden.astype(jnp.bfloat16).reshape(frames_dev, patch_dev, width)
    grad_space = lax.all_to_all(dhidden, "space", split_axis=2, concat_axis=1, tiled=True)
    dq_space, dv_space = lax.map(
        lambda quad: attend_backward(quad[0], quad[1], quad[2], quad[3]),
        (space_q, space_k, space_v, grad_space),
    )
    dq_s, dv_s = (
        lax.all_to_all(dq_space, "space", split_axis=1, concat_axis=2, tiled=True),
        lax.all_to_all(dv_space, "space", split_axis=1, concat_axis=2, tiled=True),
    )
    gb_sq, dcodes_sq = token_grads(codes_sq, dq_s, 0)
    gb_sv, dcodes_sv = token_grads(codes_sv, dv_s, 1)
    ga_sq = down_grad(inputs, dcodes_sq)
    ga_sv = down_grad(inputs, dcodes_sv)
    total_a, total_b = lax.psum(
        (jnp.stack([ga_sq, ga_sv, ga_tq, ga_tv]), jnp.stack([gb_sq, gb_sv, gb_tq, gb_tv])),
        ("dp", "tm", "space"),
    )
    grads_a = total_a * factor
    grads_b = total_b * factor
    return (mixed[None], grads_a, grads_b)


def solution(mesh):
    in_specs = (
        P("dp", "tm", "space", None),
        P("dp", "tm", "space", None),
        P("dp", "tm", "space", None),
        P("dp", "tm", "space", None),
        P("dp", "tm", "space", None),
        P("dp", "tm", "space", None),
        P("dp", "tm", "space", None),
        P(),
        P(),
        P("dp", "tm", "space", None),
    )
    out_specs = (P("dp", "tm", "space", None), P(), P())
    return jax.shard_map(
        per_device, mesh=mesh, in_specs=in_specs, out_specs=out_specs, check_vma=False
    )
```

profile of v0, /device:TPU:1, one launch (start us, length us, event | category | flops | bytes accessed | tf_op | source)
XLA Modules:
  0.0 790.9 jit_solution(8196783240402455022)
XLA Ops:
  11.5 7.6 all-to-all-start
  23.3 3.6 all-to-all-done
  32.8 5.4 all-to-all-done.1
  43.4 5.9 all-to-all-done.2
  50.3 4.9 while.22
  63.1 5.8 all-to-all-done.3
  68.8 20.7 %all-to-all-start.6 = ((bf16[4,2,18432]{2,1,0:T(2,128)(2,1)}), bf16[4,2,18432]{2,1,0:T(2,128)(2,1)S(1)}, u32[]{:S(2)}, u32[]{:S(2)}) async-start(bf16[4,2,18432]{2,1,0:T(2,128)(2,1)} %reshape.290), calls=%async_computation.6 | async-start | bytes 589824 | tf_op jit(solution)/shard_map/all_to_all | solution.py:99
  96.9 7.1 all-to-all-done.6
  104.7 5.0 all-to-all-start.8
  115.4 8.7 %all-to-all-done.8 = bf16[4,2,18432]{2,1,0:T(2,128)(2,1)} async-done(((bf16[4,2,18432]{2,1,0:T(2,128)(2,1)}), bf16[4,2,18432]{2,1,0:T(2,128)(2,1)}, u32[]{:S(2)}, u32[]{:S(2)}) %all-to-all-start.8) | async-done | bytes 294944 | tf_op jit(solution)/shard_map/all_to_all | solution.py:106
  124.1 14.4 %all-to-all-start.5 = ((bf16[4,2,18432]{2,1,0:T(2,128)(2,1)}), bf16[4,2,18432]{2,1,0:T(2,128)(2,1)}, u32[]{:S(2)}, u32[]{:S(2)}) async-start(bf16[4,2,18432]{2,1,0:T(2,128)(2,1)} %reshape.288), calls=%async_computation.5 | async-start | bytes 589824 | tf_op jit(solution)/shard_map/all_to_all | solution.py:98
  144.1 8.8 %all-to-all-done.5 = bf16[4,2,18432]{2,1,0:T(2,128)(2,1)} async-done(((bf16[4,2,18432]{2,1,0:T(2,128)(2,1)}), bf16[4,2,18432]{2,1,0:T(2,128)(2,1)}, u32[]{:S(2)}, u32[]{:S(2)}) %all-to-all-start.5) | async-done | bytes 294944 | tf_op jit(solution)/shard_map/all_to_all | solution.py:98
  152.9 5.0 all-to-all-start.4
  184.1 12.0 %all-to-all-start.10 = ((bf16[8,64,288]{2,1,0:T(8,128)(2,1)}), bf16[8,64,288]{2,1,0:T(8,128)(2,1)}, u32[]{:S(2)}, u32[]{:S(2)}) async-start(bf16[8,64,288]{2,1,0:T(8,128)(2,1)} %copy.170), calls=%async_computation.10 | async-start | bytes 786432 | tf_op jit(solution)/shard_map/all_to_all | solution.py:112
  205.4 4.3 fusion.67
  213.8 12.1 %all-to-all-start.9 = ((bf16[8,64,288]{2,1,0:T(8,128)(2,1)}), bf16[8,64,288]{2,1,0:T(8,128)(2,1)}, u32[]{:S(2)}, u32[]{:S(2)}) async-start(bf16[8,64,288]{2,1,0:T(8,128)(2,1)} %copy.166), calls=%async_computation.9 | async-start | bytes 786432 | tf_op jit(solution)/shard_map/all_to_all | solution.py:111
  228.2 13.3 %all-to-all-done.9 = bf16[8,64,288]{2,1,0:T(8,128)(2,1)} async-done(((bf16[8,64,288]{2,1,0:T(8,128)(2,1)}), bf16[8,64,288]{2,1,0:T(8,128)(2,1)}, u32[]{:S(2)}, u32[]{:S(2)}) %all-to-all-start.9) | async-done | bytes 294944 | tf_op jit(solution)/shard_map/all_to_all | solution.py:111
  247.4 4.2 all-to-all-start.11
  259.4 14.6 %all-to-all-start.7 = ((bf16[8,64,288]{2,1,0:T(8,128)(2,1)}), bf16[8,64,288]{2,1,0:T(8,128)(2,1)S(1)}, u32[]{:S(2)}, u32[]{:S(2)}) async-start(bf16[8,64,288]{2,1,0:T(8,128)(2,1)} %copy.155), calls=%async_computation.7 | async-start | bytes 786432 | tf_op jit(solution)/shard_map/all_to_all | solution.py:103
  276.6 10.1 %while.23 = (s32[]{:T(128)}, bf16[2,1024,72]{1,2,0:T(8,128)(2,1)S(1)}, bf16[2,1024,72]{1,2,0:T(8,128)(2,1)S(1)}, bf16[2,1024,72]{2,1,0:T(8,128)(2,1)S(1)}, bf16[...) while((s32[]{:T(128)}, ...), condition=%wide.region_11.12_spmd, body=%wide.region_7.11_spmd.sunk | while | flops 626144256 | bytes 33636500 | solution.py:126
  289.4 3.6 all-to-all-start.13
  295.8 6.1 all-to-all-done.13
  309.0 5.5 all-to-all-done.12
  319.0 461.6 %all-reduce.3.cloned.1.call-done = (f32[4,1152,16]{1,2,0:T(8,128)}, f32[4,16,1152]{2,1,0:T(8,128)}) async-done(((f32[4,1152,16]{1,2,0:T(8,128)}, f32[4,16,1152]{2,1,0:T(8,128)}), (f32[4,1152,16]{1,2,0:T(8,128)}, f32[4,16,1152]{2,1,0:T(8,128)})) %all-reduce.3.cloned.1.call-update) | async-done | bytes 589840 | tf_op jit(solution)/shard_map/psum | solution.py:138
  (179 shorter events, 141.0 us)
Async XLA Ops:
  7.2 23.3 %copy-start.10 = (bf16[1,2,64,1152]{3,2,1,0:T(8,128)(2,1)S(1)}, bf16[1,2,64,1152]{3,2,1,0:T(8,128)(2,1)}, u32[]{:S(2)}) copy-start(bf16[1,2,64,1152]{3,2,1,0:T(8,128)(2,1)} %param.16) | copy-start | bytes 884740
  11.5 15.4 %all-to-all-start = ((bf16[16,2,4608]{2,1,0:T(2,128)(2,1)}), bf16[16,2,4608]{2,1,0:T(2,128)(2,1)S(1)}, u32[]{:S(2)}, u32[]{:S(2)}) async-start(bf16[16,2,4608]{2,1,0:T(2,128)(2,1)} %reshape.280), calls=%async_computation | async-start | bytes 589824 | tf_op jit(solution)/shard_map/all_to_all | solution.py:86
  20.2 22.4 %copy-start.13 = (bf16[128,16]{0,1:T(8,128)(2,1)}, bf16[128,16]{0,1:T(8,128)(2,1)S(1)}, u32[]{:S(2)}) copy-start(bf16[128,16]{0,1:T(8,128)(2,1)S(1)} %convolution_convert_fusion.9) | copy-start | bytes 12292
  26.9 11.2 %all-to-all-start.1 = ((bf16[16,2,4608]{2,1,0:T(2,128)(2,1)}), bf16[16,2,4608]{2,1,0:T(2,128)(2,1)S(1)}, u32[]{:S(2)}, u32[]{:S(2)}) async-start(bf16[16,2,4608]{2,1,0:T(2,128)(2,1)} %reshape.282), calls=%async_computation.1 | async-start | bytes 589824 | tf_op jit(solution)/shard_map/all_to_all | solution.py:84
  38.1 11.2 %all-to-all-start.2 = ((bf16[16,2,4608]{2,1,0:T(2,128)(2,1)}), bf16[16,2,4608]{2,1,0:T(2,128)(2,1)S(1)}, u32[]{:S(2)}, u32[]{:S(2)}) async-start(bf16[16,2,4608]{2,1,0:T(2,128)(2,1)} %reshape.284), calls=%async_computation.2 | async-start | bytes 589824 | tf_op jit(solution)/shard_map/all_to_all | solution.py:85
  56.3 12.5 %all-to-all-start.3 = ((bf16[2,1024,72]{2,0,1:T(2,128)(2,1)}), bf16[2,1024,72]{2,0,1:T(2,128)(2,1)S(1)}, u32[]{:S(2)}, u32[]{:S(2)}) async-start(bf16[2,1024,72]{2,0,1:T(2,128)(2,1)} %copy.135), calls=%async_computation.3 | async-start | bytes 1048576 | tf_op jit(solution)/shard_map/all_to_all | solution.py:91
  68.8 35.1 %all-to-all-start.6 = ((bf16[4,2,18432]{2,1,0:T(2,128)(2,1)}), bf16[4,2,18432]{2,1,0:T(2,128)(2,1)S(1)}, u32[]{:S(2)}, u32[]{:S(2)}) async-start(bf16[4,2,18432]{2,1,0:T(2,128)(2,1)} %reshape.290), calls=%async_computation.6 | async-start | bytes 589824 | tf_op jit(solution)/shard_map/all_to_all | solution.py:99
  91.1 18.6 %copy-start = (bf16[1,2,64,1152]{3,2,1,0:T(8,128)(2,1)S(1)}, bf16[1,2,64,1152]{3,2,1,0:T(8,128)(2,1)}, u32[]{:S(2)}) copy-start(bf16[1,2,64,1152]{3,2,1,0:T(8,128)(2,1)} %param.14) | copy-start | bytes 884740
  92.7 18.0 %copy-start.5 = (bf16[4,16,1152]{2,1,0:T(8,128)(2,1)S(1)}, bf16[4,16,1152]{2,1,0:T(8,128)(2,1)}, u32[]{:S(2)}) copy-start(bf16[4,16,1152]{2,1,0:T(8,128)(2,1)} %param.22) | copy-start | bytes 442372
  104.7 19.4 %all-to-all-start.8 = ((bf16[4,2,18432]{2,1,0:T(2,128)(2,1)}), bf16[4,2,18432]{2,1,0:T(2,128)(2,1)}, u32[]{:S(2)}, u32[]{:S(2)}) async-start(bf16[4,2,18432]{2,1,0:T(2,128)(2,1)} %reshape.292), calls=%async_computation.8 | async-start | bytes 589824 | tf_op jit(solution)/shard_map/all_to_all | solution.py:106
  124.1 28.8 %all-to-all-start.5 = ((bf16[4,2,18432]{2,1,0:T(2,128)(2,1)}), bf16[4,2,18432]{2,1,0:T(2,128)(2,1)}, u32[]{:S(2)}, u32[]{:S(2)}) async-start(bf16[4,2,18432]{2,1,0:T(2,128)(2,1)} %reshape.288), calls=%async_computation.5 | async-start | bytes 589824 | tf_op jit(solution)/shard_map/all_to_all | solution.py:98
  139.4 27.1 %copy-start.17 = (bf16[128,16]{0,1:T(8,128)(2,1)}, bf16[128,16]{0,1:T(8,128)(2,1)S(1)}, u32[]{:S(2)}) copy-start(bf16[128,16]{0,1:T(8,128)(2,1)S(1)} %convolution_convert_fusion.8) | copy-start | bytes 12292
  152.9 31.2 %all-to-all-start.4 = ((bf16[4,2,18432]{2,1,0:T(2,128)(2,1)}), bf16[4,2,18432]{2,1,0:T(2,128)(2,1)}, u32[]{:S(2)}, u32[]{:S(2)}) async-start(bf16[4,2,18432]{2,1,0:T(2,128)(2,1)} %reshape.286), calls=%async_computation.4 | async-start | bytes 589824 | tf_op jit(solution)/shard_map/all_to_all | solution.py:100
  184.1 29.7 %all-to-all-start.10 = ((bf16[8,64,288]{2,1,0:T(8,128)(2,1)}), bf16[8,64,288]{2,1,0:T(8,128)(2,1)}, u32[]{:S(2)}, u32[]{:S(2)}) async-start(bf16[8,64,288]{2,1,0:T(8,128)(2,1)} %copy.170), calls=%async_computation.10 | async-start | bytes 786432 | tf_op jit(solution)/shard_map/all_to_all | solution.py:112
  213.8 27.7 %all-to-all-start.9 = ((bf16[8,64,288]{2,1,0:T(8,128)(2,1)}), bf16[8,64,288]{2,1,0:T(8,128)(2,1)}, u32[]{:S(2)}, u32[]{:S(2)}) async-start(bf16[8,64,288]{2,1,0:T(8,128)(2,1)} %copy.166), calls=%async_computation.9 | async-start | bytes 786432 | tf_op jit(solution)/shard_map/all_to_all | solution.py:111
  228.2 25.3 %copy-start.19 = (bf16[128,16]{0,1:T(8,128)(2,1)}, bf16[128,16]{0,1:T(8,128)(2,1)S(1)}, u32[]{:S(2)}) copy-start(bf16[128,16]{0,1:T(8,128)(2,1)S(1)} %convolution_convert_fusion.5) | copy-start | bytes 12292
  247.4 11.9 %all-to-all-start.11 = ((bf16[16,2,4608]{2,1,0:T(2,128)(2,1)}), bf16[16,2,4608]{2,1,0:T(2,128)(2,1)}, u32[]{:S(2)}, u32[]{:S(2)}) async-start(bf16[16,2,4608]{2,1,0:T(2,128)(2,1)} %reshape.294), calls=%async_computation.11 | async-start | bytes 589824 | tf_op jit(solution)/shard_map/all_to_all | solution.py:125
  259.4 30.0 %all-to-all-start.7 = ((bf16[8,64,288]{2,1,0:T(8,128)(2,1)}), bf16[8,64,288]{2,1,0:T(8,128)(2,1)S(1)}, u32[]{:S(2)}, u32[]{:S(2)}) async-start(bf16[8,64,288]{2,1,0:T(8,128)(2,1)} %copy.155), calls=%async_computation.7 | async-start | bytes 786432 | tf_op jit(solution)/shard_map/all_to_all | solution.py:103
  276.5 16.4 %copy-start.20 = (bf16[128,16]{0,1:T(8,128)(2,1)S(1)}, bf16[128,16]{0,1:T(8,128)(2,1)}, u32[]{:S(2)}) copy-start(bf16[128,16]{0,1:T(8,128)(2,1)} %copy-done.19) | copy-start | bytes 12292
  289.4 12.5 %all-to-all-start.13 = ((bf16[2,1024,72]{2,0,1:T(2,128)(2,1)}), bf16[2,1024,72]{2,0,1:T(2,128)(2,1)S(1)}, u32[]{:S(2)}, u32[]{:S(2)}) async-start(bf16[2,1024,72]{2,0,1:T(2,128)(2,1)} %copy.177), calls=%async_computation.13 | async-start | bytes 1048576 | tf_op jit(solution)/shard_map/all_to_all | solution.py:132
  293.7 14.6 %copy-start.16 = (bf16[128,16]{0,1:T(8,128)(2,1)S(1)}, bf16[128,16]{0,1:T(8,128)(2,1)}, u32[]{:S(2)}) copy-start(bf16[128,16]{0,1:T(8,128)(2,1)} %copy-done.15) | copy-start | bytes 12292
  293.7 14.8 %copy-start.6 = (bf16[4,16,1152]{2,1,0:T(8,128)(2,1)S(1)}, bf16[4,16,1152]{2,1,0:T(8,128)(2,1)}, u32[]{:S(2)}) copy-start(bf16[4,16,1152]{2,1,0:T(8,128)(2,1)} %param.22) | copy-start | bytes 442372
  301.9 12.5 %all-to-all-start.12 = ((bf16[2,1024,72]{2,0,1:T(2,128)(2,1)}), bf16[2,1024,72]{2,0,1:T(2,128)(2,1)S(1)}, u32[]{:S(2)}, u32[]{:S(2)}) async-start(bf16[2,1024,72]{2,0,1:T(2,128)(2,1)} %copy.174), calls=%async_computation.12 | async-start | bytes 1048576 | tf_op jit(solution)/shard_map/all_to_all | solution.py:131
  305.5 475.2 %all-reduce.3.cloned.1.call-start = ((), (), s32[]{:S(2)}) async-start(), calls=%async_computation.14 | async-start | bytes 1179648 | tf_op jit(solution)/shard_map/psum | solution.py:138
  (15 other events, 75.6 us)
Sparse Core Ops, SparseCore 0:
  318.4 462.2 all-reduce.2
where the time goes:
time: 794 us; the launch traced here: 791 us
  waiting for transfers between devices  537 us (68%)
  starting transfers between devices  114 us (14%)
  local copies, waits for them, and re-layouts  72.7 us (9%)
  matrix products  43.3 us (5%)
  between operations  14.6 us (2%)
  other arithmetic  9.65 us (1%)
    psum x1, waiting for transfers between devices, per_device(): lax.psum((jnp.stack([ga_sq, ga_sv, ga_tq, ga_tv]), jnp.stack([gb_sq, gb_s...  462 us
    unnamed x62, local copies, waits for them, and re-layouts  23 us
    all_to_all x1, starting transfers between devices, per_device(): lax.all_to_all(key_t[0], 'tm', split_axis=2, concat_axis=0, tiled=True)  20.7 us
  transfers between devices with their start and end apart: 15, of which 13 were waited for; matrix products, arithmetic and copies ran while one was open for 13% of the time, Pallas kernels for 0%

commit v1 on v0

v1 whole, which is shorter than its diff:
```python
import math

import jax
import jax.numpy as jnp
from jax import lax
from jax.experimental import pallas as pl
from jax.experimental.pallas import tpu as pltpu
from jax.sharding import PartitionSpec as P

MESH = pl.DeviceIdType.MESH
F32 = jnp.float32
BF16 = jnp.bfloat16

HEAD_DIM = 72
HEADS = 16
D = HEADS * HEAD_DIM
TOK = 128
LENGTH = 1024
CHUNK = 256
SOURCES = 4
ZCHUNKS = 8
ZHEADS = HEADS // ZCHUNKS
SCALE = HEAD_DIM ** -0.5
FACTOR = 65536 ** -0.5
LOG2E = math.log2(math.e)

NN = (((1,), (0,)), ((), ()))
NT = (((1,), (1,)), ((), ()))
TN = (((0,), (0,)), ((), ()))


def dot(a, b, dims=NN):
    return lax.dot_general(a, b, dims, preferred_element_type=F32)


def rounded(x):
    return x.astype(BF16).astype(F32)


def half_turn(x):
    return pltpu.roll(x, 64, 1)


def low_lanes():
    return lax.broadcasted_iota(jnp.int32, (1, TOK), 1) < 64


def to_frames(a, b):
    low = low_lanes()
    return jnp.where(low, a, half_turn(b)), jnp.where(low, half_turn(a), b)


def from_frames(first, second):
    low = low_lanes()
    return jnp.where(low, first, half_turn(second)), jnp.where(low, half_turn(first), second)


def head_rows(h):
    return pl.ds(pl.multiple_of(h * HEAD_DIM, 8), HEAD_DIM)


def kernel(
    patches, query_s, key_s, value_s, query_t, key_t, value_t, cot, at, bm, ah, bh,
    mixed, ga, gb,
    t0, t1, xt, qtt, cott, ht, lv, dq5,
    send_in, recv_in, codes_all, codes_own,
    kt, kn, vt, vn, qt, cf, cc, probs, ot,
    o_send, o_recv,
    kv, ctv, dcv, dcv_own,
    dct_own, dct_all, dctf, gf, dq, dv, dcs_send, dcs_recv,
    gt_send, gt_recv, za_t, zb_t, ag_t,
    gs_send, gs_recv, za_s, zb_s, ag_s,
    s_in, r_in, s_code, r_code, s_o, r_o,
    s_z, r_z, s_sib, r_sib, s_fwd, r_fwd,
    s_ctv, r_ctv, s_dcv, r_dcv, s_dct, r_dct, s_dcs, r_dcs,
    s_gt, r_gt, s_zat, r_zat, s_zbt, r_zbt, s_agt, r_agt,
    s_gs, r_gs, s_zas, r_zas, s_zbs, r_zbs, s_ags, r_ags,
):
    dp, tm, sp = lax.axis_index("dp"), lax.axis_index("tm"), lax.axis_index("space")
    z_hi, core = tm // 2, tm % 2
    d_hi, d_lo = dp // 4, dp % 4
    pos_a, pos_b = d_lo * 2 + core, z_hi * 2 + d_hi

    def space_peer(step):
        peer = (sp + step) % 16
        return peer, (dp, tm, peer)

    def tm_peer(step):
        peer = (tm + step) % 4
        return peer, (dp, peer, sp)

    def a_peer(step):
        peer = (pos_a + step) % 8
        return peer, (d_hi * 4 + peer // 2, z_hi * 2 + peer % 2, sp)

    def b_peer(step):
        peer = (pos_b + step) % 4
        return peer, ((peer % 2) * 4 + d_lo, (peer // 2) * 2 + core, sp)

    across = (tm + 2) % 4
    sibling = z_hi * 2 + 1 - core
    far = (1 - z_hi) * 2 + 1 - core

    def copy(src, dst, s_sem, r_sem, device):
        return pltpu.make_async_remote_copy(
            src_ref=src, dst_ref=dst, send_sem=s_sem, recv_sem=r_sem, device_id=device, device_id_type=MESH
        )

    def start_all(peer_of, count, src_of, dst, s_sems, r_sems, me):
        @pl.loop(1, count)
        def _(step):
            peer, device = peer_of(step)
            copy(src_of(peer), dst.at[me], s_sems.at[peer], r_sems.at[me], device).start()

    def finish_all(peer_of, count, src_of, dst, s_sems, r_sems):
        @pl.loop(1, count)
        def _(step):
            peer, device = peer_of(step)
            done = copy(src_of(peer), dst.at[peer], s_sems.at[peer], r_sems.at[peer], device)
            done.wait_recv()
            done.wait_send()

    barrier = pltpu.get_barrier_semaphore()

    @pl.loop(1, 16)
    def _(step):
        pl.semaphore_signal(barrier, inc=1, device_id=space_peer(step)[1], device_id_type=MESH)

    @pl.loop(1, 8)
    def _(step):
        pl.semaphore_signal(barrier, inc=1, device_id=a_peer(step)[1], device_id_type=MESH)

    @pl.loop(1, 4)
    def _(step):
        pl.semaphore_signal(barrier, inc=1, device_id=b_peer(step)[1], device_id_type=MESH)

    pl.semaphore_signal(barrier, inc=1, device_id=(dp, far, sp), device_id_type=MESH)

    def transpose_in(src, dst):
        for i in range(D // 128):
            dst[pl.ds(i * 128, 128), :] = src[:, pl.ds(i * 128, 128)].astype(F32).T

    transpose_in(key_t, t0)
    transpose_in(value_t, t1)

    @pl.loop(0, HEADS)
    def _(h):
        rows = head_rows(h)
        kv[tm, h] = jnp.concatenate([t0[rows, :], t1[rows, :]], axis=0).astype(BF16)

    codes_own[...] = dot(at[pl.ds(0, 32), :], patches[...], NT).astype(BF16)
    transpose_in(key_s, t0)
    transpose_in(query_s, t1)

    @pl.loop(0, HEADS)
    def _(h):
        rows = head_rows(h)
        send_in[0, h] = jnp.concatenate([t0[rows, :], t1[rows, :]], axis=0).astype(BF16)

    pl.semaphore_wait(barrier, 15 + 7 + 3 + 1)

    def z_slot(source, c):
        return kv.at[source, pl.ds(c * ZHEADS, ZHEADS)]

    for c in range(ZCHUNKS):
        copy(z_slot(tm, c), z_slot(tm, c), s_z.at[c], r_z.at[c], (dp, across, sp)).start()
    start_all(space_peer, 16, lambda p: codes_own, codes_all, s_code, r_code, sp)
    start_all(space_peer, 16, lambda p: send_in.at[0, p], recv_in.at[0], s_in.at[0], r_in.at[0], sp)
    for c in range(ZCHUNKS):
        copy(z_slot(tm, c), z_slot(tm, c), s_sib.at[c], r_sib.at[c], (dp, sibling, sp)).start()
    transpose_in(value_s, t0)
    transpose_in(cot, cott)

    @pl.loop(0, HEADS)
    def _(h):
        rows = head_rows(h)
        send_in[1, h] = jnp.concatenate([t0[rows, :], cott[rows, :]], axis=0).astype(BF16)

    start_all(space_peer, 16, lambda p: send_in.at[1, p], recv_in.at[1], s_in.at[1], r_in.at[1], sp)
    recv_in[0, sp] = send_in[0, sp]
    recv_in[1, sp] = send_in[1, sp]
    codes_all[sp] = codes_own[...]
    transpose_in(patches, xt)
    transpose_in(query_t, qtt)

    finish_all(space_peer, 16, lambda p: codes_own, codes_all, s_code, r_code)
    for part in range(2):
        finish_all(
            space_peer, 16, lambda p: send_in.at[part, p], recv_in.at[part], s_in.at[part], r_in.at[part]
        )

    @pl.loop(0, 8)
    def _(j):
        lanes = pl.ds(pl.multiple_of(j * 128, 128), 128)
        even, odd = 2 * j, 2 * j + 1
        kq = to_frames(recv_in[0, even].astype(F32), recv_in[0, odd].astype(F32))
        vc = to_frames(recv_in[1, even].astype(F32), recv_in[1, odd].astype(F32))
        codes = to_frames(codes_all[even].astype(F32), codes_all[odd].astype(F32))
        for f in range(2):
            code = codes[f].astype(BF16)
            cc[f, :, lanes] = code
            keys = kq[f][:HEAD_DIM]
            query = kq[f][HEAD_DIM:] + dot(bh[pl.ds(0, 16), :], code[:16], TN)
            values = rounded(vc[f][:HEAD_DIM] + dot(bh[pl.ds(16, 16), :], code[16:], TN))
            kt[f, :, lanes] = keys.astype(BF16)
            kn[f, lanes, :] = keys.T.astype(BF16)
            qt[f, :, lanes] = query.astype(BF16)
            vt[f, :, lanes] = values.astype(BF16)
            vn[f, lanes, :] = values.T.astype(BF16)
            cf[f, :, lanes] = vc[f][HEAD_DIM:]

    @pl.loop(0, 2 * LENGTH // CHUNK)
    def _(i):
        f = i // (LENGTH // CHUNK)
        lanes = pl.ds(pl.multiple_of((i % (LENGTH // CHUNK)) * CHUNK, CHUNK), CHUNK)
        scores = dot(kn[f], qt[f, :, lanes])
        weights = jnp.exp2((scores - jnp.max(scores, axis=0, keepdims=True)) * (SCALE * LOG2E))
        p = weights * (1.0 / jnp.sum(weights, axis=0, keepdims=True))
        probs[f, :, lanes] = p
        ot[f, :, lanes] = dot(vt[f], p.astype(BF16))

    @pl.loop(0, 8)
    def _(j):
        lanes = pl.ds(pl.multiple_of(j * 128, 128), 128)
        pair = from_frames(ot[0, :, lanes], ot[1, :, lanes])
        for k in range(2):
            o_send[2 * j + k] = jnp.concatenate([pair[k], jnp.zeros((8, TOK), F32)], axis=0).astype(BF16)

    start_all(space_peer, 16, lambda p: o_send.at[p], o_recv, s_o, r_o, sp)
    o_recv[sp] = o_send[sp]
    finish_all(space_peer, 16, lambda p: o_send.at[p], o_recv, s_o, r_o)

    @pl.loop(0, HEADS)
    def _(h):
        rows = head_rows(h)
        ht[rows, :] = rounded(xt[rows, :] + o_recv[h].astype(F32)[:HEAD_DIM])

    hidden = ht[...].astype(BF16)
    codes_t = dot(at[pl.ds(32, 32), :], hidden).astype(BF16)
    codes_tq = codes_t[:16]
    ctv[tm] = codes_t[16:]
    start_all(tm_peer, 4, lambda p: ctv.at[tm], ctv, s_ctv, r_ctv, tm)
    qtt[...] = rounded(qtt[...] + dot(bm[pl.ds(32, 16), :], codes_tq, TN))
    finish_all(tm_peer, 4, lambda p: ctv.at[tm], ctv, s_ctv, r_ctv)
    for s in range(SOURCES):
        lv[s] = dot(bm[pl.ds(48, 16), :], ctv[s], TN)

    def temporal_head(h):
        rows = head_rows(h)
        q, g = qtt[rows, :], cott[rows, :]
        keys, values, straight, turned, d_straight, d_turned = [], [], [], [], [], []
        for s in range(SOURCES):
            both = kv[s, h].astype(F32)
            k, v = both[:HEAD_DIM], rounded(both[HEAD_DIM:] + lv[s, rows, :])
            k_r, v_r = half_turn(k), half_turn(v)
            keys.append((k, k_r))
            values.append((v, v_r))
            straight.append(jnp.sum(q * k, axis=0, keepdims=True))
            turned.append(jnp.sum(q * k_r, axis=0, keepdims=True))
            d_straight.append(jnp.sum(g * v, axis=0, keepdims=True))
            d_turned.append(jnp.sum(g * v_r, axis=0, keepdims=True))
        scores = jnp.concatenate(straight + turned, axis=0)
        weights = jnp.exp2((scores - jnp.max(scores, axis=0, keepdims=True)) * (SCALE * LOG2E))
        p = weights * (1.0 / jnp.sum(weights, axis=0, keepdims=True))
        dprob = jnp.concatenate(d_straight + d_turned, axis=0)
        inner = jnp.sum(p * dprob, axis=0, keepdims=True)
        dscore = rounded(p * (dprob - inner) * SCALE)
        low = rounded(p)
        low_r, g_r = half_turn(low), half_turn(g)
        out = jnp.zeros((HEAD_DIM, TOK), F32)
        dquery = jnp.zeros((HEAD_DIM, TOK), F32)
        for s in range(SOURCES):
            out = out + low[s : s + 1] * values[s][0] + low[s + 4 : s + 5] * values[s][1]
            dquery = dquery + dscore[s : s + 1] * keys[s][0] + dscore[s + 4 : s + 5] * keys[s][1]
            dq5[1 + s, rows, :] = low[s : s + 1] * g + low_r[s + 4 : s + 5] * g_r
        dq5[0, rows, :] = dquery
        t0[rows, :] = ht[rows, :] + rounded(out)

    for c in range(ZCHUNKS):
        copy(z_slot(tm, c), z_slot(across, c), s_z.at[c], r_z.at[c], (dp, across, sp)).wait_recv()
        copy(z_slot(across, c), z_slot(across, c), s_fwd.at[c], r_fwd.at[c], (dp, sibling, sp)).start()
        copy(z_slot(tm, c), z_slot(sibling, c), s_sib.at[c], r_sib.at[c], (dp, sibling, sp)).wait_recv()
        copy(z_slot(across, c), z_slot(far, c), s_fwd.at[c], r_fwd.at[c], (dp, sibling, sp)).wait_recv()

        @pl.loop(c * ZHEADS, (c + 1) * ZHEADS)
        def _(h):
            temporal_head(h)

    for s in range(SOURCES):
        dcv_own[s] = dot(bm[pl.ds(48, 16), :], dq5[1 + s].astype(BF16))
    start_all(tm_peer, 4, lambda p: dcv_own.at[p], dcv, s_dcv, r_dcv, tm)
    dcv[tm] = dcv_own[tm]
    dq_t = dq5[0].astype(BF16)
    dcodes_tq = dot(bm[pl.ds(32, 16), :], dq_t)
    grad_b = [dot(codes_tq, dq_t, NT)]
    part_v = dot(ctv[0], dq5[1].astype(BF16), NT)
    for s in range(1, SOURCES):
        part_v = part_v + dot(ctv[s], dq5[1 + s].astype(BF16), NT)
    grad_b.append(part_v)
    finish_all(tm_peer, 4, lambda p: dcv_own.at[p], dcv, s_dcv, r_dcv)
    dcodes_tv = dcv[0] + dcv[1] + dcv[2] + dcv[3]
    dcodes_t = jnp.concatenate([dcodes_tq, dcodes_tv], axis=0).astype(BF16)
    dct_own[...] = dcodes_t
    start_all(space_peer, 16, lambda p: dct_own, dct_all, s_dct, r_dct, sp)
    dct_all[sp] = dcodes_t

    grad_a = dot(dcodes_t, ht[...].astype(BF16), NT)
    quarters = [grad_a[:16], grad_a[16:], grad_b[0], grad_b[1]]
    for r in range(4):
        for c in range(3):
            gt_send[3 * r + c] = quarters[r][:, 384 * c : 384 * (c + 1)].astype(BF16)
    for piece in range(12, 16):
        gt_send[piece] = jnp.zeros((16, 384), BF16)
    start_all(space_peer, 16, lambda p: gt_send.at[p], gt_recv, s_gt, r_gt, sp)
    gt_recv[sp] = gt_send[sp]

    for i in range(D // 128):
        cols = pl.ds(i * 128, 128)
        mixed[:, cols] = t0[cols, :].T.astype(BF16)

    finish_all(space_peer, 16, lambda p: dct_own, dct_all, s_dct, r_dct)

    @pl.loop(0, 8)
    def _(j):
        lanes = pl.ds(pl.multiple_of(j * 128, 128), 128)
        codes = to_frames(dct_all[2 * j].astype(F32), dct_all[2 * j + 1].astype(F32))
        for f in range(2):
            gf[f, :, lanes] = (
                cf[f, :, lanes] + dot(ah[pl.ds(32, 32), :], codes[f].astype(BF16), TN)
            ).astype(BF16)

    dv[...] = jnp.zeros_like(dv)

    @pl.loop(0, 2 * LENGTH // CHUNK)
    def _(i):
        f = i // (LENGTH // CHUNK)
        lanes = pl.ds(pl.multiple_of((i % (LENGTH // CHUNK)) * CHUNK, CHUNK), CHUNK)
        g = gf[f, :, lanes]
        dprob = dot(vn[f], g)
        p = probs[f, :, lanes]
        inner = jnp.sum(p * dprob, axis=0, keepdims=True)
        dscore = (p * (dprob - inner) * SCALE).astype(BF16)
        dq[f, :, lanes] = dot(kt[f], dscore)
        dv[f] += dot(g, p.astype(BF16), NT)

    def sum_slots(ref, count):
        total = ref[0].astype(F32)
        for k in range(1, count):
            total = total + ref[k].astype(F32)
        return total

    finish_all(space_peer, 16, lambda p: gt_send.at[p], gt_recv, s_gt, r_gt)
    za_t[pos_a] = sum_slots(gt_recv, 16).astype(BF16)
    start_all(a_peer, 8, lambda p: za_t.at[pos_a], za_t, s_zat, r_zat, pos_a)

    pad = jnp.zeros((128 - HEAD_DIM, LENGTH), F32)
    gb_q = jnp.zeros((16, 128), F32)
    gb_v = jnp.zeros((16, 128), F32)
    for f in range(2):
        dq_f = jnp.concatenate([dq[f], pad], axis=0).astype(BF16)
        dv_f = jnp.concatenate([dv[f], pad], axis=0).astype(BF16)
        gb_q = gb_q + dot(cc[f, pl.ds(0, 16), :], dq_f, NT)
        gb_v = gb_v + dot(cc[f, pl.ds(16, 16), :], dv_f, NT)
        dctf[f, pl.ds(0, 16), :] = dot(bh[pl.ds(0, 16), :], dq[f].astype(BF16))
        dctf[f, pl.ds(16, 16), :] = dot(bh[pl.ds(16, 16), :], dv[f].astype(BF16))

    @pl.loop(0, 8)
    def _(j):
        lanes = pl.ds(pl.multiple_of(j * 128, 128), 128)
        pair = from_frames(dctf[0, :, lanes], dctf[1, :, lanes])
        dcs_send[2 * j] = pair[0].astype(BF16)
        dcs_send[2 * j + 1] = pair[1].astype(BF16)

    start_all(space_peer, 16, lambda p: dcs_send.at[p], dcs_recv, s_dcs, r_dcs, sp)
    dcs_recv[sp] = dcs_send[sp]

    finish_all(a_peer, 8, lambda p: za_t.at[pos_a], za_t, s_zat, r_zat)
    zb_t[pos_b] = sum_slots(za_t, 8).astype(BF16)
    start_all(b_peer, 4, lambda p: zb_t.at[pos_b], zb_t, s_zbt, r_zbt, pos_b)

    finish_all(space_peer, 16, lambda p: dcs_send.at[p], dcs_recv, s_dcs, r_dcs)
    dcodes_s = sum_slots(dcs_recv, 16).astype(BF16)
    grad_s = dot(dcodes_s, patches[...])
    for r in range(2):
        for c in range(3):
            gs_send[3 * r + c] = grad_s[16 * r : 16 * (r + 1), 384 * c : 384 * (c + 1)].astype(BF16)

    @pl.when(sp < 6)
    def _():
        gs_recv[sp] = gs_send[sp]

    @pl.loop(1, 16)
    def _(step):
        peer, device = space_peer(step)

        @pl.when(peer < 6)
        def _():
            copy(gs_send.at[peer], gs_recv.at[sp], s_gs.at[peer], r_gs.at[sp], device).start()

    finish_all(b_peer, 4, lambda p: zb_t.at[pos_b], zb_t, s_zbt, r_zbt)
    ag_t[sp] = sum_slots(zb_t, 4).astype(BF16)
    start_all(space_peer, 16, lambda p: ag_t.at[sp], ag_t, s_agt, r_agt, sp)

    za_s[pos_a, :, pl.ds(384, 128)] = gb_q.astype(BF16)
    za_s[pos_a, :, pl.ds(512, 128)] = gb_v.astype(BF16)

    @pl.when(sp < 6)
    def _():
        @pl.loop(1, 16)
        def _(step):
            peer, device = space_peer(step)
            copy(gs_send.at[0], gs_recv.at[peer], s_gs.at[0], r_gs.at[peer], device).wait_recv()

        za_s[pos_a, :, pl.ds(0, 384)] = sum_slots(gs_recv, 16).astype(BF16)

    @pl.when(sp >= 6)
    def _():
        za_s[pos_a, :, pl.ds(0, 384)] = jnp.zeros((16, 384), BF16)

    start_all(a_peer, 8, lambda p: za_s.at[pos_a], za_s, s_zas, r_zas, pos_a)

    @pl.loop(1, 16)
    def _(step):
        peer, device = space_peer(step)

        @pl.when(peer < 6)
        def _():
            copy(gs_send.at[peer], gs_recv.at[sp], s_gs.at[peer], r_gs.at[sp], device).wait_send()

    finish_all(a_peer, 8, lambda p: za_s.at[pos_a], za_s, s_zas, r_zas)
    zb_s[pos_b] = sum_slots(za_s, 8).astype(BF16)
    start_all(b_peer, 4, lambda p: zb_s.at[pos_b], zb_s, s_zbs, r_zbs, pos_b)
    finish_all(space_peer, 16, lambda p: ag_t.at[sp], ag_t, s_agt, r_agt)
    for r in range(4):
        for c in range(3):
            out = ga if r < 2 else gb
            piece = ag_t[3 * r + c].astype(F32) * FACTOR
            out[pl.ds(32 + 16 * (r % 2), 16), pl.ds(384 * c, 384)] = piece
    for c in range(ZCHUNKS):
        copy(z_slot(tm, c), z_slot(tm, c), s_z.at[c], r_z.at[c], (dp, across, sp)).wait_send()
        copy(z_slot(tm, c), z_slot(tm, c), s_sib.at[c], r_sib.at[c], (dp, sibling, sp)).wait_send()
        copy(z_slot(across, c), z_slot(across, c), s_fwd.at[c], r_fwd.at[c], (dp, sibling, sp)).wait_send()
    finish_all(b_peer, 4, lambda p: zb_s.at[pos_b], zb_s, s_zbs, r_zbs)
    ag_s[sp] = sum_slots(zb_s, 4).astype(BF16)
    start_all(space_peer, 16, lambda p: ag_s.at[sp], ag_s, s_ags, r_ags, sp)
    finish_all(space_peer, 16, lambda p: ag_s.at[sp], ag_s, s_ags, r_ags)
    for r in range(2):
        for c in range(3):
            piece = ag_s[3 * r + c, :, pl.ds(0, 384)].astype(F32) * FACTOR
            ga[pl.ds(16 * r, 16), pl.ds(384 * c, 384)] = piece
    for r in range(2):
        tiles = [jnp.zeros((16, 128), F32) for _ in range(D // 128)]
        for h in range(HEADS):
            first, offset = divmod(h * HEAD_DIM, 128)
            piece = ag_s[h, :, pl.ds(384 + 128 * r, 128)].astype(F32) * FACTOR
            if offset:
                piece = pltpu.roll(piece, offset, 1)
            lane = lax.broadcasted_iota(jnp.int32, (1, 128), 1)
            tiles[first] = tiles[first] + jnp.where(lane >= offset, piece, 0.0)
            if offset + HEAD_DIM > 128:
                tiles[first + 1] = tiles[first + 1] + jnp.where(lane < offset, piece, 0.0)
        for i in range(D // 128):
            gb[pl.ds(16 * r, 16), pl.ds(128 * i, 128)] = tiles[i]


def scratch():
    def f32(*shape):
        return pltpu.VMEM(shape, F32)

    def bf16(*shape):
        return pltpu.VMEM(shape, BF16)

    def sems(*shape):
        return pltpu.SemaphoreType.DMA(shape)

    whole = f32(D, TOK)
    return [
        whole, whole, whole, whole, whole, whole, f32(SOURCES, D, TOK), f32(1 + SOURCES, D, TOK),
        bf16(2, HEADS, 144, TOK), bf16(2, HEADS, 144, TOK), bf16(HEADS, 32, TOK), bf16(32, TOK),
        bf16(2, HEAD_DIM, LENGTH), bf16(2, LENGTH, HEAD_DIM), bf16(2, HEAD_DIM, LENGTH), bf16(2, LENGTH, HEAD_DIM),
        bf16(2, HEAD_DIM, LENGTH), f32(2, HEAD_DIM, LENGTH), bf16(2, 32, LENGTH), f32(2, LENGTH, LENGTH),
        f32(2, HEAD_DIM, LENGTH),
        bf16(HEADS, 80, TOK), bf16(HEADS, 80, TOK),
        bf16(SOURCES, HEADS, 144, TOK), bf16(SOURCES, 16, TOK), f32(SOURCES, 16, TOK), f32(SOURCES, 16, TOK),
        bf16(32, TOK), bf16(HEADS, 32, TOK), f32(2, 32, LENGTH), bf16(2, HEAD_DIM, LENGTH),
        f32(2, HEAD_DIM, LENGTH), f32(2, HEAD_DIM, LENGTH), bf16(HEADS, 32, TOK), bf16(HEADS, 32, TOK),
        bf16(16, 16, 384), bf16(16, 16, 384), bf16(8, 16, 384), bf16(4, 16, 384), bf16(16, 16, 384),
        bf16(6, 16, 384), bf16(16, 16, 384), bf16(8, 16, 640), bf16(4, 16, 640), bf16(16, 16, 640),
        sems(2, 16), sems(2, 16), sems(16), sems(16), sems(16), sems(16),
        sems(ZCHUNKS), sems(ZCHUNKS), sems(ZCHUNKS), sems(ZCHUNKS), sems(ZCHUNKS), sems(ZCHUNKS),
        sems(4), sems(4), sems(4), sems(4), sems(16), sems(16), sems(16), sems(16),
        sems(16), sems(16), sems(8), sems(8), sems(4), sems(4), sems(16), sems(16),
        sems(16), sems(16), sems(8), sems(8), sems(4), sems(4), sems(16), sems(16),
    ]


def per_device(
    patches, query_s, key_s, value_s, query_t, key_t, value_t, adapters_a, adapters_b, cotangent
):
    at = jnp.swapaxes(adapters_a, 1, 2).reshape(64, D)
    bm = adapters_b.reshape(64, D)
    start = lax.axis_index("space") * HEAD_DIM
    ah = lax.dynamic_slice_in_dim(at, start, HEAD_DIM, axis=1)
    bh = lax.dynamic_slice_in_dim(bm, start, HEAD_DIM, axis=1)
    tokens = [
        array.reshape(TOK, D)
        for array in (patches, query_s, key_s, value_s, query_t, key_t, value_t, cotangent)
    ]
    mixed, ga, gb = pl.pallas_call(
        kernel,
        out_shape=(
            jax.ShapeDtypeStruct((TOK, D), BF16),
            jax.ShapeDtypeStruct((64, D), F32),
            jax.ShapeDtypeStruct((64, D), F32),
        ),
        in_specs=[pl.BlockSpec(memory_space=pltpu.VMEM)] * 12,
        out_specs=[pl.BlockSpec(memory_space=pltpu.VMEM)] * 3,
        scratch_shapes=scratch(),
        compiler_params=pltpu.CompilerParams(
            collective_id=0, has_side_effects=True, vmem_limit_bytes=56 * 1024 * 1024
        ),
    )(*tokens, at, bm, ah, bh)
    grads_a = jnp.swapaxes(ga.reshape(4, 16, D), 1, 2)
    grads_b = gb.reshape(4, 16, D)
    return mixed.reshape(patches.shape), grads_a, grads_b


def solution(mesh):
    tokens = P("dp", "tm", "space", None)
    return jax.shard_map(
        per_device,
        mesh=mesh,
        in_specs=(tokens,) * 7 + (P(), P(), tokens),
        out_specs=(tokens, P(), P()),
        check_vma=False,
    )
```

time: 794 us -> 153 us (0.19)
  waiting for transfers between devices: 537 us -> 0 us
  Pallas kernels: 0 us -> 147 us
  starting transfers between devices: 114 us -> 0 us
  local copies, waits for them, and re-layouts: 72.7 us -> 5 us
  matrix products: 43.3 us -> 0 us
  between operations: 14.6 us -> 0.65 us
  other arithmetic: 9.65 us -> 0 us
    psum x1 -> x0, waiting for transfers between devices: 462 us -> none  [per_device(): lax.psum((jnp.stack([ga_sq, ga_sv, ga_tq, ga_tv]), jnp.stack([gb_sq, gb_s...]
    pallas_call x0 -> x1, Pallas kernels: none -> 147 us  [per_device(): pl.pallas_call(kernel, out_shape=(jax.ShapeDtypeStruct((TOK, D), BF16), j...]
    all_to_all x14 -> x0, starting transfers between devices: 113 us -> none  [the longest x1 20.7 us: per_device(): lax.all_to_all(key_t[0], 'tm', split_axis=2, concat_axis=0, tiled=True)]
    all_to_all x14 -> x0, waiting for transfers between devices: 75.2 us -> none  [the longest x1 13.3 us: per_device(): lax.all_to_all(dq_time, 'tm', split_axis=0, concat_axis=2, tiled=True)]
    dot_general x36 -> x0, matrix products: 39.9 us -> none  [the longest x3 7.13 us: attend_backward(): jnp.einsum('hqk,khd->qhd', dscore, heads_k, preferred_element_type=jnp.fl...]
    unnamed x62 -> x7, local copies, waits for them, and re-layouts: 23 us -> 3.53 us
    all_to_all x17 -> x0, local copies, waits for them, and re-layouts: 19.1 us -> none  [the longest x2 3.62 us: per_device(): lax.all_to_all(q_t, 'tm', split_axis=2, concat_axis=0, tiled=True)]
    reshape x13 -> x0, local copies, waits for them, and re-layouts: 12.5 us -> none  [the longest x4 4.49 us: adapted(): return lifted.astype(jnp.bfloat16).reshape(frames_dev, patch_dev, width)]
  transfers between devices with their start and end apart: 15 -> 0, of which waited for: 13 -> 0; matrix products, arithmetic and copies ran while one was open for 13% -> 0% of each run, Pallas kernels for 0% -> 0%
where the time goes in v1:
time: 153 us
  Pallas kernels  147 us (96%)
  local copies, waits for them, and re-layouts  5 us (3%)
    pallas_call x1, Pallas kernels, per_device(): pl.pallas_call(kernel, out_shape=(jax.ShapeDtypeStruct((TOK, D), BF16), j...  147 us
    unnamed x7, local copies, waits for them, and re-layouts  3.53 us

profile of v1, /device:TPU:1, one launch (start us, length us, event | category | flops | bytes accessed | tf_op | source)
XLA Modules:
  0.0 152.9 jit_solution(10057349380451915035)
XLA Ops:
  0.6 1.5 constant_dynamic-slice_fusion
  2.1 147.2 %shard_map.121 = (bf16[128,1152]{1,0:T(8,128)(2,1)}, f32[64,1152]{1,0:T(8,128)}, f32[64,1152]{1,0:T(8,128)}) custom-call(bf16[128,1152]{1,0:T(8,128)(2,1)} %bitcast.20, bf16[128,1152]{1,0:T(8,128)(2,1)} %bitcast.21, bf16[128,1152]{1,0:T(8,128)(2,1)} %bitcast.22, bf16[128,1152]{1,0:T(8,128)(2,1)} %bitcast.23, bf16[128,1152]{1,0:T(8,128)(2,1)} %bitcast.24, ...), custom_call_target="tpu_custom_call" | custom-call | tf_op jit(solution)/shard_map/pallas_call | solution.py:509
  149.3 0.0 copy-start.1
  149.3 1.7 %copy.16 = bf16[1,2,64,1152]{3,2,1,0:T(8,128)(2,1)} copy(bf16[1,2,64,1152]{3,2,1,0:T(8,128)(2,1)} %bitcast.19) | data formatting | bytes 589824
  151.1 0.0 copy-done.1
  151.1 0.0 copy-start
  151.1 0.7 copy.17
  151.8 0.4 copy-done
  152.2 0.7 copy.18
Async XLA Ops:
  149.3 1.8 %copy-start.1 = (f32[64,1152]{1,0:T(8,128)S(1)}, f32[64,1152]{1,0:T(8,128)}, u32[]{:S(2)}) copy-start(f32[64,1152]{1,0:T(8,128)} %get-tuple-element.7) | copy-start | bytes 884740
  151.1 1.1 copy-start

commit v2 on v1

v2 whole, which is shorter than its diff:
```python
import math

import jax
import jax.numpy as jnp
from jax import lax
from jax.experimental import pallas as pl
from jax.experimental.pallas import tpu as pltpu
from jax.sharding import PartitionSpec as P

MESH = pl.DeviceIdType.MESH
F32 = jnp.float32
BF16 = jnp.bfloat16

HEAD_DIM = 72
HEADS = 16
D = HEADS * HEAD_DIM
TOK = 128
LENGTH = 1024
CHUNK = 256
SOURCES = 4
ZCHUNKS = 8
ZHEADS = HEADS // ZCHUNKS
PIECES = 18
SCALE = HEAD_DIM ** -0.5
FACTOR = 65536 ** -0.5
LOG2E = math.log2(math.e)

NN = (((1,), (0,)), ((), ()))
NT = (((1,), (1,)), ((), ()))
TN = (((0,), (0,)), ((), ()))


def dot(a, b, dims=NN):
    return lax.dot_general(a, b, dims, preferred_element_type=F32)


def rounded(x):
    return x.astype(BF16).astype(F32)


def half_turn(x):
    return pltpu.roll(x, 64, 1)


def low_lanes():
    return lax.broadcasted_iota(jnp.int32, (1, TOK), 1) < 64


def to_frames(a, b):
    low = low_lanes()
    return jnp.where(low, a, half_turn(b)), jnp.where(low, half_turn(a), b)


def from_frames(first, second):
    low = low_lanes()
    return jnp.where(low, first, half_turn(second)), jnp.where(low, half_turn(first), second)


def head_rows(h):
    return pl.ds(pl.multiple_of(h * HEAD_DIM, 8), HEAD_DIM)


def kernel(
    patches_hbm, query_s_hbm, key_s_hbm, value_s_hbm, query_t_hbm, key_t_hbm, value_t_hbm, cot_hbm, at_hbm, bm_hbm,
    mixed, ga, gb,
    patches, query_s, key_s, value_s, query_t, key_t, value_t, cot, at, bm, s_load,
    ah, bh, abt, t0, t1, xt, qtt, cott, ht, lv, dq5,
    send_in, recv_in, codes_all, codes_own,
    kt, kn, vt, vn, qt, cf, cc, probs, probs_low, ot, oe,
    o_send, o_recv,
    kv, ctv, dcv, dcv_own,
    dct_own, dct_all, dctf, gf, dq, dv, dcs_send, dcs_recv,
    gt_send, gt_recv, z_t, ag_t,
    gs_send, gs_recv, gb_send, gb_recv, z_s, ag_s,
    s_in, r_in, s_code, r_code, s_o, r_o,
    s_z, r_z, s_sib, r_sib, s_fwd, r_fwd,
    s_ctv, r_ctv, s_dcv, r_dcv, s_dct, r_dct, s_dcs, r_dcs,
    s_gt, r_gt, s_zt, r_zt, s_agt, r_agt,
    s_gs, r_gs, s_gb, r_gb, s_zs, r_zs, s_ags, r_ags,
):
    dp, tm, sp = lax.axis_index("dp"), lax.axis_index("tm"), lax.axis_index("space")
    z_hi, core = tm // 2, tm % 2
    z = z_hi * 8 + dp
    block = sp * 2 + core

    def space_peer(step):
        peer = (sp + step) % 16
        return peer, (dp, tm, peer)

    def tm_peer(step):
        peer = (tm + step) % 4
        return peer, (dp, peer, sp)

    def block_peer(step):
        peer = (block + step) % 32
        return peer, (dp, z_hi * 2 + peer % 2, peer // 2)

    def z_peer(step):
        peer = (z + step) % 16
        return peer, (peer % 8, (peer // 8) * 2 + core, sp)

    across = (tm + 2) % 4
    sibling = z_hi * 2 + 1 - core
    far = (1 - z_hi) * 2 + 1 - core

    def copy(src, dst, s_sem, r_sem, device):
        return pltpu.make_async_remote_copy(
            src_ref=src, dst_ref=dst, send_sem=s_sem, recv_sem=r_sem, device_id=device, device_id_type=MESH
        )

    def start_all(peer_of, count, src_of, dst, s_sem, r_sem, me, limit=None):
        @pl.loop(1, count)
        def _(step):
            peer, device = peer_of(step)

            def start():
                copy(src_of(peer), dst.at[me], s_sem, r_sem, device).start()

            if limit is None:
                start()
            else:
                pl.when(peer < limit)(start)

    def sent_all(peer_of, count, src_of, dst, s_sem, r_sem, me, limit=None):
        def wait(slots):
            all_slots = dst.at[pl.ds(0, slots)]
            copy(all_slots, all_slots, s_sem, r_sem, peer_of(1)[1]).wait_send()

        if limit is None:
            wait(count - 1)
        else:
            pl.when(me < limit)(lambda: wait(limit - 1))
            pl.when(me >= limit)(lambda: wait(limit))

    def received_all(peer_of, count, src_of, dst, s_sem, r_sem, me, limit=None):
        def wait(slots):
            all_slots = dst.at[pl.ds(0, slots)]
            copy(all_slots, all_slots, s_sem, r_sem, peer_of(1)[1]).wait_recv()

        if limit is None:
            wait(count - 1)
        else:
            pl.when(me < limit)(lambda: wait(limit - 1))
            pl.when(me >= limit)(lambda: wait(limit))

    barrier = pltpu.get_barrier_semaphore()
    pl.semaphore_signal(barrier, inc=1, device_id=(dp, far, sp), device_id_type=MESH)

    @pl.loop(1, 16)
    def _(step):
        pl.semaphore_signal(barrier, inc=1, device_id=z_peer(step)[1], device_id_type=MESH)

    @pl.loop(1, 32)
    def _(step):
        pl.semaphore_signal(barrier, inc=1, device_id=block_peer(step)[1], device_id_type=MESH)

    loads = {}
    for i, (src, dst) in enumerate((
        (key_t_hbm, key_t), (value_t_hbm, value_t), (patches_hbm, patches), (at_hbm, at), (key_s_hbm, key_s),
        (query_s_hbm, query_s), (value_s_hbm, value_s), (cot_hbm, cot), (bm_hbm, bm), (query_t_hbm, query_t),
    )):
        loads[id(dst)] = pltpu.make_async_copy(src, dst, s_load.at[i])
        loads[id(dst)].start()

    def transpose_in(src, dst):
        loads[id(src)].wait()
        for i in range(D // 128):
            dst[pl.ds(i * 128, 128), :] = src[:, pl.ds(i * 128, 128)].astype(F32).T

    transpose_in(key_t, t0)
    transpose_in(value_t, t1)

    @pl.loop(0, HEADS)
    def _(h):
        rows = head_rows(h)
        kv[tm, h] = jnp.concatenate([t0[rows, :], t1[rows, :]], axis=0).astype(BF16)

    loads[id(patches)].wait()
    loads[id(at)].wait()
    codes_own[...] = dot(at[pl.ds(0, 32), :], patches[...], NT).astype(BF16)
    transpose_in(key_s, t0)
    transpose_in(query_s, t1)

    @pl.loop(0, HEADS)
    def _(h):
        rows = head_rows(h)
        send_in[0, h] = jnp.concatenate([t0[rows, :], t1[rows, :]], axis=0).astype(BF16)

    pl.semaphore_wait(barrier, 1 + 15 + 31)

    def z_slot(source, c):
        return kv.at[source, pl.ds(c * ZHEADS, ZHEADS)]

    for c in range(ZCHUNKS):
        copy(z_slot(tm, c), z_slot(tm, c), s_z, r_z.at[c], (dp, across, sp)).start()
    codes_x = (space_peer, 16, lambda p: codes_own, codes_all, s_code, r_code, sp)
    start_all(*codes_x)
    in_x = [
        (space_peer, 16, lambda p: send_in.at[0, p], recv_in.at[0], s_in.at[0], r_in.at[0], sp),
        (space_peer, 16, lambda p: send_in.at[1, p], recv_in.at[1], s_in.at[1], r_in.at[1], sp),
    ]
    start_all(*in_x[0])
    own_to_sibling = copy(kv.at[tm], kv.at[tm], s_sib, r_sib, (dp, sibling, sp))
    own_to_sibling.start()
    transpose_in(value_s, t0)
    transpose_in(cot, cott)

    @pl.loop(0, HEADS)
    def _(h):
        rows = head_rows(h)
        send_in[1, h] = jnp.concatenate([t0[rows, :], cott[rows, :]], axis=0).astype(BF16)

    start_all(*in_x[1])
    recv_in[0, sp] = send_in[0, sp]
    recv_in[1, sp] = send_in[1, sp]
    codes_all[sp] = codes_own[...]
    for i in range(D // 128):
        xt[pl.ds(i * 128, 128), :] = patches[:, pl.ds(i * 128, 128)].astype(F32).T
    transpose_in(query_t, qtt)
    loads[id(bm)].wait()
    for src, dst in ((at, ah), (bm, bh)):
        for i in range(D // 128):
            abt[pl.ds(i * 128, 128), :] = src[:, pl.ds(i * 128, 128)].astype(F32).T
        dst[...] = abt[head_rows(sp), :].T.astype(BF16)

    received_all(*codes_x)
    received_all(*in_x[0])
    received_all(*in_x[1])

    @pl.loop(0, 8)
    def _(j):
        lanes = pl.ds(pl.multiple_of(j * 128, 128), 128)
        even, odd = 2 * j, 2 * j + 1
        kq = to_frames(recv_in[0, even].astype(F32), recv_in[0, odd].astype(F32))
        vc = to_frames(recv_in[1, even].astype(F32), recv_in[1, odd].astype(F32))
        codes = to_frames(codes_all[even].astype(F32), codes_all[odd].astype(F32))
        for f in range(2):
            code = codes[f].astype(BF16)
            cc[f, :, lanes] = code
            keys = kq[f][:HEAD_DIM]
            query = kq[f][HEAD_DIM:] + dot(bh[pl.ds(0, 16), :], code[:16], TN)
            values = rounded(vc[f][:HEAD_DIM] + dot(bh[pl.ds(16, 16), :], code[16:], TN))
            kt[f, :, lanes] = keys.astype(BF16)
            kn[f, lanes, :] = keys.T.astype(BF16)
            qt[f, :, lanes] = query.astype(BF16)
            vt[f, :, lanes] = values.astype(BF16)
            vn[f, lanes, :] = values.T.astype(BF16)
            cf[f, :, lanes] = vc[f][HEAD_DIM:]

    @pl.loop(0, 2 * LENGTH // CHUNK)
    def _(i):
        f = i // (LENGTH // CHUNK)
        lanes = pl.ds(pl.multiple_of((i % (LENGTH // CHUNK)) * CHUNK, CHUNK), CHUNK)
        scores = dot(kn[f], qt[f, :, lanes])
        weights = jnp.exp2((scores - jnp.max(scores, axis=0, keepdims=True)) * (SCALE * LOG2E))
        p = weights * (1.0 / jnp.sum(weights, axis=0, keepdims=True))
        low = p.astype(BF16)
        probs[f, :, lanes] = p * SCALE
        probs_low[f, :, lanes] = low
        out = dot(vt[f], low)
        ot[f, :, lanes] = out
        oe[f, :, lanes] = out + dot(vt[f], (p - low.astype(F32)).astype(BF16))

    @pl.loop(0, 8)
    def _(j):
        lanes = pl.ds(pl.multiple_of(j * 128, 128), 128)
        pair = from_frames(ot[0, :, lanes], ot[1, :, lanes])
        for k in range(2):
            o_send[2 * j + k] = jnp.concatenate([pair[k], jnp.zeros((8, TOK), F32)], axis=0).astype(BF16)

    o_x = (space_peer, 16, lambda p: o_send.at[p], o_recv, s_o, r_o, sp)
    start_all(*o_x)
    o_recv[sp] = o_send[sp]
    sent_all(*codes_x)
    sent_all(*in_x[0])
    sent_all(*in_x[1])
    received_all(*o_x)

    @pl.loop(0, HEADS)
    def _(h):
        rows = head_rows(h)
        ht[rows, :] = rounded(xt[rows, :] + o_recv[h].astype(F32)[:HEAD_DIM])

    hidden = ht[...].astype(BF16)
    codes_t = dot(at[pl.ds(32, 32), :], hidden).astype(BF16)
    codes_tq = codes_t[:16]
    ctv[tm] = codes_t[16:]
    ctv_x = (tm_peer, 4, lambda p: ctv.at[tm], ctv, s_ctv, r_ctv, tm)
    start_all(*ctv_x)
    sent_all(*o_x)
    qtt[...] = rounded(qtt[...] + dot(bm[pl.ds(32, 16), :], codes_tq, TN))
    received_all(*ctv_x)
    for s in range(SOURCES):
        lv[s] = dot(bm[pl.ds(48, 16), :], ctv[s], TN)

    def temporal_head(h):
        rows = head_rows(h)
        q, g = qtt[rows, :], cott[rows, :]
        keys, values, straight, turned, d_straight, d_turned = [], [], [], [], [], []
        for s in range(SOURCES):
            both = kv[s, h].astype(F32)
            k, v = both[:HEAD_DIM], rounded(both[HEAD_DIM:] + lv[s, rows, :])
            k_r, v_r = half_turn(k), half_turn(v)
            keys.append((k, k_r))
            values.append((v, v_r))
            straight.append(jnp.sum(q * k, axis=0, keepdims=True))
            turned.append(jnp.sum(q * k_r, axis=0, keepdims=True))
            d_straight.append(jnp.sum(g * v, axis=0, keepdims=True))
            d_turned.append(jnp.sum(g * v_r, axis=0, keepdims=True))
        scores = jnp.concatenate(straight + turned, axis=0)
        weights = jnp.exp2((scores - jnp.max(scores, axis=0, keepdims=True)) * (SCALE * LOG2E))
        p = weights * (1.0 / jnp.sum(weights, axis=0, keepdims=True))
        dprob = jnp.concatenate(d_straight + d_turned, axis=0)
        inner = jnp.sum(p * dprob, axis=0, keepdims=True)
        dscore = rounded(p * (dprob - inner) * SCALE)
        low = rounded(p)
        low_r, g_r = half_turn(low), half_turn(g)
        out = jnp.zeros((HEAD_DIM, TOK), F32)
        dquery = jnp.zeros((HEAD_DIM, TOK), F32)
        for s in range(SOURCES):
            out = out + low[s : s + 1] * values[s][0] + low[s + 4 : s + 5] * values[s][1]
            dquery = dquery + dscore[s : s + 1] * keys[s][0] + dscore[s + 4 : s + 5] * keys[s][1]
            dq5[1 + s, rows, :] = low[s : s + 1] * g + low_r[s + 4 : s + 5] * g_r
        dq5[0, rows, :] = dquery
        t0[rows, :] = ht[rows, :] + rounded(out)

    own_to_sibling.wait_recv()
    for c in range(ZCHUNKS):
        copy(z_slot(tm, c), z_slot(across, c), s_z, r_z.at[c], (dp, across, sp)).wait_recv()
        copy(z_slot(across, c), z_slot(across, c), s_fwd, r_fwd.at[c], (dp, sibling, sp)).start()
        copy(z_slot(across, c), z_slot(far, c), s_fwd, r_fwd.at[c], (dp, sibling, sp)).wait_recv()

        @pl.loop(c * ZHEADS, (c + 1) * ZHEADS)
        def _(h):
            temporal_head(h)

    for s in range(SOURCES):
        dcv_own[s] = dot(bm[pl.ds(48, 16), :], dq5[1 + s].astype(BF16))
    dcv_x = (tm_peer, 4, lambda p: dcv_own.at[p], dcv, s_dcv, r_dcv, tm)
    start_all(*dcv_x)
    sent_all(*ctv_x)
    dcv[tm] = dcv_own[tm]
    dq_t = dq5[0].astype(BF16)
    dcodes_tq = dot(bm[pl.ds(32, 16), :], dq_t)
    grad_b = [dot(codes_tq, dq_t, NT)]
    part_v = dot(ctv[0], dq5[1].astype(BF16), NT)
    for s in range(1, SOURCES):
        part_v = part_v + dot(ctv[s], dq5[1 + s].astype(BF16), NT)
    grad_b.append(part_v)
    copy(kv.at[tm], kv.at[tm], s_z, r_z.at[0], (dp, across, sp)).wait_send()
    own_to_sibling.wait_send()
    copy(kv.at[across], kv.at[across], s_fwd, r_fwd.at[0], (dp, sibling, sp)).wait_send()
    received_all(*dcv_x)
    dcodes_tv = dcv[0] + dcv[1] + dcv[2] + dcv[3]
    dcodes_t = jnp.concatenate([dcodes_tq, dcodes_tv], axis=0).astype(BF16)
    dct_own[...] = dcodes_t
    dct_x = (space_peer, 16, lambda p: dct_own, dct_all, s_dct, r_dct, sp)
    start_all(*dct_x)
    dct_all[sp] = dcodes_t

    grad_a = dot(dcodes_t, ht[...].astype(BF16), NT)
    halves = [grad_a, jnp.concatenate(grad_b, axis=0)]
    for r in range(2):
        for c in range(9):
            gt_send[9 * r + c] = halves[r][:, 128 * c : 128 * (c + 1)].astype(BF16)
    gt_x = (block_peer, 32, lambda p: gt_send.at[p], gt_recv, s_gt, r_gt, block, PIECES)
    start_all(*gt_x)

    for i in range(D // 128):
        cols = pl.ds(i * 128, 128)
        mixed[:, cols] = t0[cols, :].T.astype(BF16)

    sent_all(*dcv_x)
    received_all(*dct_x)

    @pl.loop(0, 8)
    def _(j):
        lanes = pl.ds(pl.multiple_of(j * 128, 128), 128)
        codes = to_frames(dct_all[2 * j].astype(F32), dct_all[2 * j + 1].astype(F32))
        for f in range(2):
            gf[f, :, lanes] = (
                cf[f, :, lanes] + dot(ah[pl.ds(32, 32), :], codes[f].astype(BF16), TN)
            ).astype(BF16)

    dv[...] = jnp.zeros_like(dv)

    def backward(f):
        @pl.loop(0, LENGTH // CHUNK)
        def _(i):
            lanes = pl.ds(pl.multiple_of(i * CHUNK, CHUNK), CHUNK)
            g = gf[f, :, lanes]
            inner = jnp.sum(g.astype(F32) * oe[f, :, lanes], axis=0, keepdims=True)
            dprob = dot(vn[f], g)
            dscore = (probs[f, :, lanes] * (dprob - inner)).astype(BF16)
            dq[f, :, lanes] = dot(kt[f], dscore)
            dv[f] += dot(g, probs_low[f, :, lanes], NT)

    def sum_slots(ref, count):
        total = ref[0].astype(F32)
        for k in range(1, count):
            total = total + ref[k].astype(F32)
        return total

    backward(0)
    z_t_x = (z_peer, 16, lambda p: z_t.at[z], z_t, s_zt, r_zt, z)

    @pl.when(block < PIECES)
    def _():
        gt_recv[block] = gt_send[block]
        received_all(block_peer, 32, lambda p: gt_send.at[p], gt_recv, s_gt, r_gt, block)
        z_t[z] = sum_slots(gt_recv, 32).astype(BF16)
        start_all(*z_t_x)

    backward(1)
    pad = jnp.zeros((128 - HEAD_DIM, LENGTH), F32)
    gb_q = jnp.zeros((16, 128), F32)
    gb_v = jnp.zeros((16, 128), F32)
    for f in range(2):
        dctf[f, pl.ds(0, 16), :] = dot(bh[pl.ds(0, 16), :], dq[f].astype(BF16))
        dctf[f, pl.ds(16, 16), :] = dot(bh[pl.ds(16, 16), :], dv[f].astype(BF16))

    @pl.loop(0, 8)
    def _(j):
        lanes = pl.ds(pl.multiple_of(j * 128, 128), 128)
        pair = from_frames(dctf[0, :, lanes], dctf[1, :, lanes])
        dcs_send[2 * j] = pair[0].astype(BF16)
        dcs_send[2 * j + 1] = pair[1].astype(BF16)

    dcs_x = (space_peer, 16, lambda p: dcs_send.at[p], dcs_recv, s_dcs, r_dcs, sp)
    start_all(*dcs_x)
    dcs_recv[sp] = dcs_send[sp]
    for f in range(2):
        dq_f = jnp.concatenate([dq[f], pad], axis=0).astype(BF16)
        dv_f = jnp.concatenate([dv[f], pad], axis=0).astype(BF16)
        gb_q = gb_q + dot(cc[f, pl.ds(0, 16), :], dq_f, NT)
        gb_v = gb_v + dot(cc[f, pl.ds(16, 16), :], dv_f, NT)
    gb_send[0] = gb_q.astype(BF16)
    gb_send[1] = gb_v.astype(BF16)
    to_sibling = copy(gb_send.at[1 - core], gb_recv, s_gb, r_gb, (dp, sibling, sp))
    to_sibling.start()
    sent_all(*dct_x)
    sent_all(*gt_x)
    received_all(*dcs_x)
    dcodes_s = sum_slots(dcs_recv, 16).astype(BF16)
    grad_s = dot(dcodes_s, patches[...])
    for r in range(2):
        for c in range(9):
            gs_send[9 * r + c] = grad_s[16 * r : 16 * (r + 1), 128 * c : 128 * (c + 1)].astype(BF16)
    gs_x = (block_peer, 32, lambda p: gs_send.at[p], gs_recv, s_gs, r_gs, block, PIECES)
    start_all(*gs_x)
    sent_all(*dcs_x)
    to_sibling.wait_recv()
    z_s[z, pl.ds(16, 16), :] = (gb_send[core].astype(F32) + gb_recv[...].astype(F32)).astype(BF16)

    @pl.when(block < PIECES)
    def _():
        received_all(*z_t_x)
        ag_t[block] = sum_slots(z_t, 16).astype(BF16)
        gs_recv[block] = gs_send[block]
        received_all(block_peer, 32, lambda p: gs_send.at[p], gs_recv, s_gs, r_gs, block)
        z_s[z, pl.ds(0, 16), :] = sum_slots(gs_recv, 32).astype(BF16)

    @pl.when(block >= PIECES)
    def _():
        z_s[z, pl.ds(0, 16), :] = jnp.zeros((16, 128), BF16)

    z_s_x = (z_peer, 16, lambda p: z_s.at[z], z_s, s_zs, r_zs, z)
    start_all(*z_s_x)
    ag_t_x = (block_peer, 32, lambda p: ag_t.at[block], ag_t, s_agt, r_agt, block)

    @pl.when(block < PIECES)
    def _():
        start_all(*ag_t_x)
        sent_all(*z_t_x)

    sent_all(*gs_x)
    to_sibling.wait_send()
    received_all(*ag_t_x, PIECES)
    for piece in range(PIECES):
        out = (ga, gb)[piece // 9]
        out[pl.ds(32, 32), pl.ds(128 * (piece % 9), 128)] = ag_t[piece].astype(F32) * FACTOR

    @pl.when(block < PIECES)
    def _():
        sent_all(*ag_t_x)

    received_all(*z_s_x)
    ag_s[block] = sum_slots(z_s, 16).astype(BF16)
    ag_s_x = (block_peer, 32, lambda p: ag_s.at[block], ag_s, s_ags, r_ags, block)
    start_all(*ag_s_x)
    sent_all(*z_s_x)
    received_all(*ag_s_x)
    for piece in range(PIECES):
        rows = pl.ds(16 * (piece // 9), 16)
        ga[rows, pl.ds(128 * (piece % 9), 128)] = ag_s[piece, pl.ds(0, 16), :].astype(F32) * FACTOR
    for r in range(2):
        tiles = [jnp.zeros((16, 128), F32) for _ in range(D // 128)]
        for h in range(HEADS):
            first, offset = divmod(h * HEAD_DIM, 128)
            piece = ag_s[2 * h + r, pl.ds(16, 16), :].astype(F32) * FACTOR
            if offset:
                piece = pltpu.roll(piece, offset, 1)
            lane = lax.broadcasted_iota(jnp.int32, (1, 128), 1)
            tiles[first] = tiles[first] + jnp.where(lane >= offset, piece, 0.0)
            if offset + HEAD_DIM > 128:
                tiles[first + 1] = tiles[first + 1] + jnp.where(lane < offset, piece, 0.0)
        for i in range(D // 128):
            gb[pl.ds(16 * r, 16), pl.ds(128 * i, 128)] = tiles[i]
    sent_all(*ag_s_x)


def scratch():
    def f32(*shape):
        return pltpu.VMEM(shape, F32)

    def bf16(*shape):
        return pltpu.VMEM(shape, BF16)

    def sems(*shape):
        return pltpu.SemaphoreType.DMA(shape)

    whole = f32(D, TOK)
    one = pltpu.SemaphoreType.DMA
    return [
        *[bf16(TOK, D)] * 8, bf16(64, D), bf16(64, D), sems(10),
        bf16(64, HEAD_DIM), bf16(64, HEAD_DIM), f32(D, 64),
        whole, whole, whole, whole, whole, whole, f32(SOURCES, D, TOK), f32(1 + SOURCES, D, TOK),
        bf16(2, HEADS, 144, TOK), bf16(2, HEADS, 144, TOK), bf16(HEADS, 32, TOK), bf16(32, TOK),
        bf16(2, HEAD_DIM, LENGTH), bf16(2, LENGTH, HEAD_DIM), bf16(2, HEAD_DIM, LENGTH), bf16(2, LENGTH, HEAD_DIM),
        bf16(2, HEAD_DIM, LENGTH), f32(2, HEAD_DIM, LENGTH), bf16(2, 32, LENGTH), f32(2, LENGTH, LENGTH),
        bf16(2, LENGTH, LENGTH), f32(2, HEAD_DIM, LENGTH), f32(2, HEAD_DIM, LENGTH),
        bf16(HEADS, 80, TOK), bf16(HEADS, 80, TOK),
        bf16(SOURCES, HEADS, 144, TOK), bf16(SOURCES, 16, TOK), f32(SOURCES, 16, TOK), f32(SOURCES, 16, TOK),
        bf16(32, TOK), bf16(HEADS, 32, TOK), f32(2, 32, LENGTH), bf16(2, HEAD_DIM, LENGTH),
        f32(2, HEAD_DIM, LENGTH), f32(2, HEAD_DIM, LENGTH), bf16(HEADS, 32, TOK), bf16(HEADS, 32, TOK),
        bf16(PIECES, 32, 128), bf16(32, 32, 128), bf16(16, 32, 128), bf16(32, 32, 128),
        bf16(PIECES, 16, 128), bf16(32, 16, 128), bf16(2, 16, 128), bf16(16, 128), bf16(16, 32, 128), bf16(32, 32, 128),
        sems(2), sems(2), one, one, one, one,
        one, sems(ZCHUNKS), one, one, one, sems(ZCHUNKS),
        one, one, one, one, one, one, one, one,
        one, one, one, one, one, one,
        one, one, one, one, one, one, one, one,
    ]


def hand_over(mixed, ga, gb, mixed_out, ga_out, gb_out):
    mixed_out[...] = mixed[...]
    ga_out[...] = ga[...]
    gb_out[...] = gb[...]


def per_device(
    patches, query_s, key_s, value_s, query_t, key_t, value_t, adapters_a, adapters_b, cotangent
):
    at = jnp.swapaxes(adapters_a, 1, 2).reshape(64, D)
    bm = adapters_b.reshape(64, D)
    tokens = [
        array.reshape(TOK, D)
        for array in (patches, query_s, key_s, value_s, query_t, key_t, value_t, cotangent)
    ]
    out_shape = (
        jax.ShapeDtypeStruct((TOK, D), BF16),
        jax.ShapeDtypeStruct((64, D), F32),
        jax.ShapeDtypeStruct((64, D), F32),
    )
    results = pl.pallas_call(
        kernel,
        out_shape=out_shape,
        in_specs=[pl.BlockSpec(memory_space=pl.ANY)] * 10,
        out_specs=[pl.BlockSpec(memory_space=pltpu.VMEM)] * 3,
        scratch_shapes=scratch(),
        compiler_params=pltpu.CompilerParams(
            collective_id=0, has_side_effects=True, vmem_limit_bytes=56 * 1024 * 1024
        ),
    )(*tokens, at, bm)
    mixed, ga, gb = pl.pallas_call(
        hand_over,
        out_shape=out_shape,
        in_specs=[pl.BlockSpec(memory_space=pltpu.VMEM)] * 3,
        out_specs=[pl.BlockSpec(memory_space=pltpu.VMEM)] * 3,
    )(*results)
    grads_a = jnp.swapaxes(ga.reshape(4, 16, D), 1, 2)
    grads_b = gb.reshape(4, 16, D)
    return mixed.reshape(patches.shape), grads_a, grads_b


def solution(mesh):
    tokens = P("dp", "tm", "space", None)
    return jax.shard_map(
        per_device,
        mesh=mesh,
        in_specs=(tokens,) * 7 + (P(), P(), tokens),
        out_specs=(tokens, P(), P()),
        check_vma=False,
    )
```

time: 153 us -> 137 us (0.90)
  Pallas kernels: 147 us -> 136 us
  local copies, waits for them, and re-layouts: 5 us -> 0 us
    pallas_call x1 -> x2, Pallas kernels: 147 us -> 136 us  [the longest x1 134 us: per_device(): pl.pallas_call(kernel, out_shape=out_shape, in_specs=[pl.BlockSpec(memory...]
    unnamed x7 -> x0, local copies, waits for them, and re-layouts: 3.53 us -> none
where the time goes in v2:
time: 137 us
  Pallas kernels  136 us (99%)
    pallas_call x1, Pallas kernels, per_device(): pl.pallas_call(kernel, out_shape=out_shape, in_specs=[pl.BlockSpec(memory...  134 us

profile of v2, /device:TPU:1, one launch (start us, length us, event | category | flops | bytes accessed | tf_op | source)
XLA Modules:
  0.0 137.0 jit_solution(610759634051867842)
XLA Ops:
  0.6 134.3 %shard_map.121 = (bf16[128,1152]{1,0:T(8,128)(2,1)}, f32[64,1152]{1,0:T(8,128)}, f32[64,1152]{1,0:T(8,128)}) custom-call(bf16[128,1152]{1,0:T(8,128)(2,1)} %bitcast.17, bf16[128,1152]{1,0:T(8,128)(2,1)} %bitcast.18, bf16[128,1152]{1,0:T(8,128)(2,1)} %bitcast.19, bf16[128,1152]{1,0:T(8,128)(2,1)} %bitcast.20, bf16[128,1152]{1,0:T(8,128)(2,1)} %bitcast.21, ...), custom_call_target="tpu_custom_call" | custom-call | tf_op jit(solution)/shard_map/pallas_call | solution.py:566
  134.9 2.1 %shard_map.122 = (bf16[128,1152]{1,0:T(8,128)(2,1)}, f32[64,1152]{1,0:T(8,128)}, f32[64,1152]{1,0:T(8,128)}) custom-call(bf16[128,1152]{1,0:T(8,128)(2,1)} %get-tuple-element.9.mixed, f32[64,1152]{1,0:T(8,128)} %get-tuple-element.10.ga, f32[64,1152]{1,0:T(8,128)} %get-tuple-element.11.gb), custom_call_target="tpu_custom_call" | custom-call | tf_op jit(solution)/shard_map/pallas_call | solution.py:576

commit v3 on v2

--- a/solution.py
+++ b/solution.py
@@ -16,7 +16,7 @@
 D = HEADS * HEAD_DIM
 TOK = 128
 LENGTH = 1024
-CHUNK = 256
+CHUNK = 1024
 SOURCES = 4
 ZCHUNKS = 8
 ZHEADS = HEADS // ZCHUNKS
@@ -65,7 +65,7 @@
     mixed, ga, gb,
     patches, query_s, key_s, value_s, query_t, key_t, value_t, cot, at, bm, s_load,
     ah, bh, abt, t0, t1, xt, qtt, cott, ht, lv, dq5,
-    send_in, recv_in, codes_all, codes_own,
+    send_kq, recv_kq, send_v, recv_v, send_c, recv_c, codes_all, codes_own,
     kt, kn, vt, vn, qt, cf, cc, probs, probs_low, ot, oe,
     o_send, o_recv,
     kv, ctv, dcv, dcv_own,
@@ -184,35 +184,41 @@
     @pl.loop(0, HEADS)
     def _(h):
         rows = head_rows(h)
-        send_in[0, h] = jnp.concatenate([t0[rows, :], t1[rows, :]], axis=0).astype(BF16)
+        send_kq[h] = jnp.concatenate([t0[rows, :], t1[rows, :]], axis=0).astype(BF16)
 
     pl.semaphore_wait(barrier, 1 + 15 + 31)
 
     def z_slot(source, c):
         return kv.at[source, pl.ds(c * ZHEADS, ZHEADS)]
 
+    def send_chunk(c):
+        copy(z_slot(tm, c), z_slot(tm, c), s_z, r_z.at[c], (dp, across, sp)).start()
+
     for c in range(ZCHUNKS):
-        copy(z_slot(tm, c), z_slot(tm, c), s_z, r_z.at[c], (dp, across, sp)).start()
+        send_chunk(c)
     codes_x = (space_peer, 16, lambda p: codes_own, codes_all, s_code, r_code, sp)
     start_all(*codes_x)
-    in_x = [
-        (space_peer, 16, lambda p: send_in.at[0, p], recv_in.at[0], s_in.at[0], r_in.at[0], sp),
-        (space_peer, 16, lambda p: send_in.at[1, p], recv_in.at[1], s_in.at[1], r_in.at[1], sp),
-    ]
-    start_all(*in_x[0])
+    kq_x = (space_peer, 16, lambda p: send_kq.at[p], recv_kq, s_in.at[0], r_in.at[0], sp)
+    v_x = (space_peer, 16, lambda p: send_v.at[p], recv_v, s_in.at[1], r_in.at[1], sp)
+    c_x = (space_peer, 16, lambda p: send_c.at[p], recv_c, s_in.at[2], r_in.at[2], sp)
+    start_all(*kq_x)
     own_to_sibling = copy(kv.at[tm], kv.at[tm], s_sib, r_sib, (dp, sibling, sp))
     own_to_sibling.start()
+    gap = jnp.zeros((8, TOK), F32)
+
+    def pack(src, dst):
+        @pl.loop(0, HEADS)
+        def _(h):
+            dst[h] = jnp.concatenate([src[head_rows(h), :], gap], axis=0).astype(BF16)
+
     transpose_in(value_s, t0)
+    pack(t0, send_v)
+    start_all(*v_x)
     transpose_in(cot, cott)
-
-    @pl.loop(0, HEADS)
-    def _(h):
-        rows = head_rows(h)
-        send_in[1, h] = jnp.concatenate([t0[rows, :], cott[rows, :]], axis=0).astype(BF16)
-
-    start_all(*in_x[1])
-    recv_in[0, sp] = send_in[0, sp]
-    recv_in[1, sp] = send_in[1, sp]
+    pack(cott, send_c)
+    recv_kq[sp] = send_kq[sp]
+    recv_v[sp] = send_v[sp]
+    recv_c[sp] = send_c[sp]
     codes_all[sp] = codes_own[...]
     for i in range(D // 128):
         xt[pl.ds(i * 128, 128), :] = patches[:, pl.ds(i * 128, 128)].astype(F32).T
@@ -224,42 +230,44 @@
         dst[...] = abt[head_rows(sp), :].T.astype(BF16)
 
     received_all(*codes_x)
-    received_all(*in_x[0])
-    received_all(*in_x[1])
+    received_all(*kq_x)
+    received_all(*v_x)
 
     @pl.loop(0, 8)
     def _(j):
         lanes = pl.ds(pl.multiple_of(j * 128, 128), 128)
         even, odd = 2 * j, 2 * j + 1
-        kq = to_frames(recv_in[0, even].astype(F32), recv_in[0, odd].astype(F32))
-        vc = to_frames(recv_in[1, even].astype(F32), recv_in[1, odd].astype(F32))
+        kq = to_frames(recv_kq[even].astype(F32), recv_kq[odd].astype(F32))
+        value = to_frames(recv_v[even].astype(F32), recv_v[odd].astype(F32))
         codes = to_frames(codes_all[even].astype(F32), codes_all[odd].astype(F32))
         for f in range(2):
             code = codes[f].astype(BF16)
             cc[f, :, lanes] = code
             keys = kq[f][:HEAD_DIM]
             query = kq[f][HEAD_DIM:] + dot(bh[pl.ds(0, 16), :], code[:16], TN)
-            values = rounded(vc[f][:HEAD_DIM] + dot(bh[pl.ds(16, 16), :], code[16:], TN))
+            values = rounded(value[f][:HEAD_DIM] + dot(bh[pl.ds(16, 16), :], code[16:], TN))
             kt[f, :, lanes] = keys.astype(BF16)
             kn[f, lanes, :] = keys.T.astype(BF16)
             qt[f, :, lanes] = query.astype(BF16)
             vt[f, :, lanes] = values.astype(BF16)
             vn[f, lanes, :] = values.T.astype(BF16)
-            cf[f, :, lanes] = vc[f][HEAD_DIM:]
-
-    @pl.loop(0, 2 * LENGTH // CHUNK)
-    def _(i):
-        f = i // (LENGTH // CHUNK)
-        lanes = pl.ds(pl.multiple_of((i % (LENGTH // CHUNK)) * CHUNK, CHUNK), CHUNK)
-        scores = dot(kn[f], qt[f, :, lanes])
-        weights = jnp.exp2((scores - jnp.max(scores, axis=0, keepdims=True)) * (SCALE * LOG2E))
-        p = weights * (1.0 / jnp.sum(weights, axis=0, keepdims=True))
-        low = p.astype(BF16)
-        probs[f, :, lanes] = p * SCALE
-        probs_low[f, :, lanes] = low
-        out = dot(vt[f], low)
-        ot[f, :, lanes] = out
-        oe[f, :, lanes] = out + dot(vt[f], (p - low.astype(F32)).astype(BF16))
+
+    def forward(f):
+        @pl.loop(0, LENGTH // CHUNK)
+        def _(i):
+            lanes = pl.ds(pl.multiple_of(i * CHUNK, CHUNK), CHUNK)
+            scores = dot(kn[f], qt[f, :, lanes])
+            weights = jnp.exp2((scores - jnp.max(scores, axis=0, keepdims=True)) * (SCALE * LOG2E))
+            p = weights * (1.0 / jnp.sum(weights, axis=0, keepdims=True))
+            low = p.astype(BF16)
+            probs[f, :, lanes] = p * SCALE
+            probs_low[f, :, lanes] = low
+            out = dot(vt[f], low)
+            ot[f, :, lanes] = out
+            oe[f, :, lanes] = out + dot(vt[f], (p - low.astype(F32)).astype(BF16))
+
+    forward(0)
+    forward(1)
 
     @pl.loop(0, 8)
     def _(j):
@@ -272,9 +280,10 @@
     start_all(*o_x)
     o_recv[sp] = o_send[sp]
     sent_all(*codes_x)
-    sent_all(*in_x[0])
-    sent_all(*in_x[1])
+    sent_all(*kq_x)
+    sent_all(*v_x)
     received_all(*o_x)
+    start_all(*c_x)
 
     @pl.loop(0, HEADS)
     def _(h):
@@ -325,9 +334,26 @@
         t0[rows, :] = ht[rows, :] + rounded(out)
 
     own_to_sibling.wait_recv()
-    for c in range(ZCHUNKS):
+
+    def relay_chunk(c):
         copy(z_slot(tm, c), z_slot(across, c), s_z, r_z.at[c], (dp, across, sp)).wait_recv()
         copy(z_slot(across, c), z_slot(across, c), s_fwd, r_fwd.at[c], (dp, sibling, sp)).start()
+
+    sent_all(*c_x)
+    received_all(*c_x)
+
+    @pl.loop(0, 8)
+    def _(j):
+        lanes = pl.ds(pl.multiple_of(j * 128, 128), 128)
+        even, odd = 2 * j, 2 * j + 1
+        grad = to_frames(recv_c[even].astype(F32), recv_c[odd].astype(F32))
+        for f in range(2):
+            cf[f, :, lanes] = grad[f][:HEAD_DIM]
+
+    relay_chunk(0)
+    for c in range(ZCHUNKS):
+        if c + 1 < ZCHUNKS:
+            relay_chunk(c + 1)
         copy(z_slot(across, c), z_slot(far, c), s_fwd, r_fwd.at[c], (dp, sibling, sp)).wait_recv()
 
         @pl.loop(c * ZHEADS, (c + 1) * ZHEADS)
@@ -376,7 +402,8 @@
     @pl.loop(0, 8)
     def _(j):
         lanes = pl.ds(pl.multiple_of(j * 128, 128), 128)
-        codes = to_frames(dct_all[2 * j].astype(F32), dct_all[2 * j + 1].astype(F32))
+        even, odd = 2 * j, 2 * j + 1
+        codes = to_frames(dct_all[even].astype(F32), dct_all[odd].astype(F32))
         for f in range(2):
             gf[f, :, lanes] = (
                 cf[f, :, lanes] + dot(ah[pl.ds(32, 32), :], codes[f].astype(BF16), TN)
@@ -478,7 +505,7 @@
     received_all(*ag_t_x, PIECES)
     for piece in range(PIECES):
         out = (ga, gb)[piece // 9]
-        out[pl.ds(32, 32), pl.ds(128 * (piece % 9), 128)] = ag_t[piece].astype(F32) * FACTOR
+        out[pl.ds(32, 32), pl.ds(128 * (piece % 9), 128)] = ag_t[piece]
 
     @pl.when(block < PIECES)
     def _():
@@ -492,12 +519,12 @@
     received_all(*ag_s_x)
     for piece in range(PIECES):
         rows = pl.ds(16 * (piece // 9), 16)
-        ga[rows, pl.ds(128 * (piece % 9), 128)] = ag_s[piece, pl.ds(0, 16), :].astype(F32) * FACTOR
+        ga[rows, pl.ds(128 * (piece % 9), 128)] = ag_s[piece, pl.ds(0, 16), :]
     for r in range(2):
         tiles = [jnp.zeros((16, 128), F32) for _ in range(D // 128)]
         for h in range(HEADS):
             first, offset = divmod(h * HEAD_DIM, 128)
-            piece = ag_s[2 * h + r, pl.ds(16, 16), :].astype(F32) * FACTOR
+            piece = ag_s[2 * h + r, pl.ds(16, 16), :].astype(F32)
             if offset:
                 piece = pltpu.roll(piece, offset, 1)
             lane = lax.broadcasted_iota(jnp.int32, (1, 128), 1)
@@ -505,7 +532,7 @@
             if offset + HEAD_DIM > 128:
                 tiles[first + 1] = tiles[first + 1] + jnp.where(lane < offset, piece, 0.0)
         for i in range(D // 128):
-            gb[pl.ds(16 * r, 16), pl.ds(128 * i, 128)] = tiles[i]
+            gb[pl.ds(16 * r, 16), pl.ds(128 * i, 128)] = tiles[i].astype(BF16)
     sent_all(*ag_s_x)
 
 
@@ -525,7 +552,8 @@
         *[bf16(TOK, D)] * 8, bf16(64, D), bf16(64, D), sems(10),
         bf16(64, HEAD_DIM), bf16(64, HEAD_DIM), f32(D, 64),
         whole, whole, whole, whole, whole, whole, f32(SOURCES, D, TOK), f32(1 + SOURCES, D, TOK),
-        bf16(2, HEADS, 144, TOK), bf16(2, HEADS, 144, TOK), bf16(HEADS, 32, TOK), bf16(32, TOK),
+        bf16(HEADS, 144, TOK), bf16(HEADS, 144, TOK), bf16(HEADS, 80, TOK), bf16(HEADS, 80, TOK),
+        bf16(HEADS, 80, TOK), bf16(HEADS, 80, TOK), bf16(HEADS, 32, TOK), bf16(32, TOK),
         bf16(2, HEAD_DIM, LENGTH), bf16(2, LENGTH, HEAD_DIM), bf16(2, HEAD_DIM, LENGTH), bf16(2, LENGTH, HEAD_DIM),
         bf16(2, HEAD_DIM, LENGTH), f32(2, HEAD_DIM, LENGTH), bf16(2, 32, LENGTH), f32(2, LENGTH, LENGTH),
         bf16(2, LENGTH, LENGTH), f32(2, HEAD_DIM, LENGTH), f32(2, HEAD_DIM, LENGTH),
@@ -535,7 +563,7 @@
         f32(2, HEAD_DIM, LENGTH), f32(2, HEAD_DIM, LENGTH), bf16(HEADS, 32, TOK), bf16(HEADS, 32, TOK),
         bf16(PIECES, 32, 128), bf16(32, 32, 128), bf16(16, 32, 128), bf16(32, 32, 128),
         bf16(PIECES, 16, 128), bf16(32, 16, 128), bf16(2, 16, 128), bf16(16, 128), bf16(16, 32, 128), bf16(32, 32, 128),
-        sems(2), sems(2), one, one, one, one,
+        sems(3), sems(3), one, one, one, one,
         one, sems(ZCHUNKS), one, one, one, sems(ZCHUNKS),
         one, one, one, one, one, one, one, one,
         one, one, one, one, one, one,
@@ -545,8 +573,8 @@
 
 def hand_over(mixed, ga, gb, mixed_out, ga_out, gb_out):
     mixed_out[...] = mixed[...]
-    ga_out[...] = ga[...]
-    gb_out[...] = gb[...]
+    ga_out[...] = ga[...].astype(F32) * FACTOR
+    gb_out[...] = gb[...].astype(F32) * FACTOR
 
 
 def per_device(
@@ -565,7 +593,11 @@
     )
     results = pl.pallas_call(
         kernel,
-        out_shape=out_shape,
+        out_shape=(
+            jax.ShapeDtypeStruct((TOK, D), BF16),
+            jax.ShapeDtypeStruct((64, D), BF16),
+            jax.ShapeDtypeStruct((64, D), BF16),
+        ),
         in_specs=[pl.BlockSpec(memory_space=pl.ANY)] * 10,
         out_specs=[pl.BlockSpec(memory_space=pltpu.VMEM)] * 3,
         scratch_shapes=scratch(),

time: 137 us -> 130 us (0.949)
  Pallas kernels: 136 us -> 129 us
    pallas_call x1, Pallas kernels: 134 us -> 127 us  [per_device(): pl.pallas_call(kernel, out_shape=(jax.ShapeDtypeStruct((TOK, D), BF16), j...]
where the time goes in v3:
time: 130 us
  Pallas kernels  129 us (99%)
    pallas_call x1, Pallas kernels, per_device(): pl.pallas_call(kernel, out_shape=(jax.ShapeDtypeStruct((TOK, D), BF16), j...  127 us

profile of v3, /device:TPU:1, one launch (start us, length us, event | category | flops | bytes accessed | tf_op | source)
XLA Modules:
  0.0 130.0 jit_solution(13071680529895734409)
XLA Ops:
  0.6 127.3 %shard_map.121 = (bf16[128,1152]{1,0:T(8,128)(2,1)}, bf16[64,1152]{1,0:T(8,128)(2,1)}, bf16[64,1152]{1,0:T(8,128)(2,1)}) custom-call(bf16[128,1152]{1,0:T(8,128)(2,1)} %bitcast.17, bf16[128,1152]{1,0:T(8,128)(2,1)} %bitcast.18, bf16[128,1152]{1,0:T(8,128)(2,1)} %bitcast.19, bf16[128,1152]{1,0:T(8,128)(2,1)} %bitcast.20, bf16[128,1152]{1,0:T(8,128)(2,1)} %bitcast.21, ...), custom_call_target="tpu_custom_call" | custom-call | tf_op jit(solution)/shard_map/pallas_call | solution.py:594
  128.0 2.0 %shard_map.122 = (bf16[128,1152]{1,0:T(8,128)(2,1)}, f32[64,1152]{1,0:T(8,128)}, f32[64,1152]{1,0:T(8,128)}) custom-call(bf16[128,1152]{1,0:T(8,128)(2,1)} %get-tuple-element.9.mixed, bf16[64,1152]{1,0:T(8,128)(2,1)} %get-tuple-element.10.ga, bf16[64,1152]{1,0:T(8,128)(2,1)} %get-tuple-element.11.gb), custom_call_target="tpu_custom_call" | custom-call | tf_op jit(solution)/shard_map/pallas_call | solution.py:608

commit v4 on v3

--- a/solution.py
+++ b/solution.py
@@ -76,12 +76,12 @@
     s_z, r_z, s_sib, r_sib, s_fwd, r_fwd,
     s_ctv, r_ctv, s_dcv, r_dcv, s_dct, r_dct, s_dcs, r_dcs,
     s_gt, r_gt, s_zt, r_zt, s_agt, r_agt,
-    s_gs, r_gs, s_gb, r_gb, s_zs, r_zs, s_ags, r_ags,
+    s_gs, r_gs, s_gb, r_gb, s_zs, r_zs, s_ags, r_ags, r_agh,
 ):
     dp, tm, sp = lax.axis_index("dp"), lax.axis_index("tm"), lax.axis_index("space")
     z_hi, core = tm // 2, tm % 2
     z = z_hi * 8 + dp
-    block = sp * 2 + core
+    block = core * 16 + sp
 
     def space_peer(step):
         peer = (sp + step) % 16
@@ -93,7 +93,7 @@
 
     def block_peer(step):
         peer = (block + step) % 32
-        return peer, (dp, z_hi * 2 + peer % 2, peer // 2)
+        return peer, (dp, z_hi * 2 + peer // 16, peer % 16)
 
     def z_peer(step):
         peer = (z + step) % 16
@@ -109,17 +109,20 @@
         )
 
     def start_all(peer_of, count, src_of, dst, s_sem, r_sem, me, limit=None):
-        @pl.loop(1, count)
-        def _(step):
-            peer, device = peer_of(step)
-
-            def start():
+        if limit is None:
+            @pl.loop(1, count)
+            def _(step):
+                peer, device = peer_of(step)
                 copy(src_of(peer), dst.at[me], s_sem, r_sem, device).start()
-
-            if limit is None:
-                start()
-            else:
-                pl.when(peer < limit)(start)
+        else:
+            @pl.loop(0, limit)
+            def _(step):
+                peer = (me + step) % limit
+
+                @pl.when(peer != me)
+                def _():
+                    device = (dp, z_hi * 2 + peer // 16, peer % 16)
+                    copy(src_of(peer), dst.at[me], s_sem, r_sem, device).start()
 
     def sent_all(peer_of, count, src_of, dst, s_sem, r_sem, me, limit=None):
         def wait(slots):
@@ -142,6 +145,12 @@
         else:
             pl.when(me < limit)(lambda: wait(limit - 1))
             pl.when(me >= limit)(lambda: wait(limit))
+
+    def sum_slots(ref, count):
+        total = ref[0].astype(F32)
+        for k in range(1, count):
+            total = total + ref[k].astype(F32)
+        return total
 
     barrier = pltpu.get_barrier_semaphore()
     pl.semaphore_signal(barrier, inc=1, device_id=(dp, far, sp), device_id_type=MESH)
@@ -361,7 +370,7 @@
             temporal_head(h)
 
     for s in range(SOURCES):
-        dcv_own[s] = dot(bm[pl.ds(48, 16), :], dq5[1 + s].astype(BF16))
+        dcv_own[s] = dot(bm[pl.ds(48, 16), :], dq5[1 + s].astype(BF16)).astype(BF16)
     dcv_x = (tm_peer, 4, lambda p: dcv_own.at[p], dcv, s_dcv, r_dcv, tm)
     start_all(*dcv_x)
     sent_all(*ctv_x)
@@ -377,7 +386,7 @@
     own_to_sibling.wait_send()
     copy(kv.at[across], kv.at[across], s_fwd, r_fwd.at[0], (dp, sibling, sp)).wait_send()
     received_all(*dcv_x)
-    dcodes_tv = dcv[0] + dcv[1] + dcv[2] + dcv[3]
+    dcodes_tv = sum_slots(dcv, SOURCES)
     dcodes_t = jnp.concatenate([dcodes_tq, dcodes_tv], axis=0).astype(BF16)
     dct_own[...] = dcodes_t
     dct_x = (space_peer, 16, lambda p: dct_own, dct_all, s_dct, r_dct, sp)
@@ -421,12 +430,6 @@
             dscore = (probs[f, :, lanes] * (dprob - inner)).astype(BF16)
             dq[f, :, lanes] = dot(kt[f], dscore)
             dv[f] += dot(g, probs_low[f, :, lanes], NT)
-
-    def sum_slots(ref, count):
-        total = ref[0].astype(F32)
-        for k in range(1, count):
-            total = total + ref[k].astype(F32)
-        return total
 
     backward(0)
     z_t_x = (z_peer, 16, lambda p: z_t.at[z], z_t, s_zt, r_zt, z)
@@ -487,12 +490,13 @@
         received_all(block_peer, 32, lambda p: gs_send.at[p], gs_recv, s_gs, r_gs, block)
         z_s[z, pl.ds(0, 16), :] = sum_slots(gs_recv, 32).astype(BF16)
 
-    @pl.when(block >= PIECES)
-    def _():
-        z_s[z, pl.ds(0, 16), :] = jnp.zeros((16, 128), BF16)
-
+    z_half = z_s.at[pl.ds(0, 16), pl.ds(16, 16)]
     z_s_x = (z_peer, 16, lambda p: z_s.at[z], z_s, s_zs, r_zs, z)
-    start_all(*z_s_x)
+    z_h_x = (z_peer, 16, lambda p: z_half.at[z], z_half, s_zs, r_zs, z)
+    has_piece = pl.when(block < PIECES)
+    no_piece = pl.when(block >= PIECES)
+    has_piece(lambda: start_all(*z_s_x))
+    no_piece(lambda: start_all(*z_h_x))
     ag_t_x = (block_peer, 32, lambda p: ag_t.at[block], ag_t, s_agt, r_agt, block)
 
     @pl.when(block < PIECES)
@@ -511,12 +515,33 @@
     def _():
         sent_all(*ag_t_x)
 
-    received_all(*z_s_x)
-    ag_s[block] = sum_slots(z_s, 16).astype(BF16)
+    ag_half = ag_s.at[pl.ds(0, 32), pl.ds(16, 16)]
     ag_s_x = (block_peer, 32, lambda p: ag_s.at[block], ag_s, s_ags, r_ags, block)
-    start_all(*ag_s_x)
-    sent_all(*z_s_x)
-    received_all(*ag_s_x)
+    ag_h_x = (block_peer, 32, lambda p: ag_half.at[block], ag_half, s_ags, r_agh, block)
+
+    @has_piece
+    def _():
+        received_all(*z_s_x)
+        ag_s[block] = sum_slots(z_s, 16).astype(BF16)
+        start_all(*ag_s_x)
+        sent_all(*z_s_x)
+        received_all(*ag_s_x, PIECES)
+        everything = ag_half.at[pl.ds(0, 32 - PIECES)]
+        copy(everything, everything, s_ags, r_agh, (dp, sibling, sp)).wait_recv()
+
+    @no_piece
+    def _():
+        received_all(*z_h_x)
+        total = z_s[0, pl.ds(16, 16), :].astype(F32)
+        for k in range(1, 16):
+            total = total + z_s[k, pl.ds(16, 16), :].astype(F32)
+        ag_s[block, pl.ds(16, 16), :] = total.astype(BF16)
+        start_all(*ag_h_x)
+        sent_all(*z_h_x)
+        received_all(*ag_s_x, PIECES)
+        others = ag_half.at[pl.ds(0, 31 - PIECES)]
+        copy(others, others, s_ags, r_agh, (dp, sibling, sp)).wait_recv()
+
     for piece in range(PIECES):
         rows = pl.ds(16 * (piece // 9), 16)
         ga[rows, pl.ds(128 * (piece % 9), 128)] = ag_s[piece, pl.ds(0, 16), :]
@@ -524,7 +549,7 @@
         tiles = [jnp.zeros((16, 128), F32) for _ in range(D // 128)]
         for h in range(HEADS):
             first, offset = divmod(h * HEAD_DIM, 128)
-            piece = ag_s[2 * h + r, pl.ds(16, 16), :].astype(F32)
+            piece = ag_s[16 * r + h, pl.ds(16, 16), :].astype(F32)
             if offset:
                 piece = pltpu.roll(piece, offset, 1)
             lane = lax.broadcasted_iota(jnp.int32, (1, 128), 1)
@@ -533,7 +558,8 @@
                 tiles[first + 1] = tiles[first + 1] + jnp.where(lane < offset, piece, 0.0)
         for i in range(D // 128):
             gb[pl.ds(16 * r, 16), pl.ds(128 * i, 128)] = tiles[i].astype(BF16)
-    sent_all(*ag_s_x)
+    has_piece(lambda: sent_all(*ag_s_x))
+    no_piece(lambda: sent_all(*ag_h_x))
 
 
 def scratch():
@@ -558,7 +584,7 @@
         bf16(2, HEAD_DIM, LENGTH), f32(2, HEAD_DIM, LENGTH), bf16(2, 32, LENGTH), f32(2, LENGTH, LENGTH),
         bf16(2, LENGTH, LENGTH), f32(2, HEAD_DIM, LENGTH), f32(2, HEAD_DIM, LENGTH),
         bf16(HEADS, 80, TOK), bf16(HEADS, 80, TOK),
-        bf16(SOURCES, HEADS, 144, TOK), bf16(SOURCES, 16, TOK), f32(SOURCES, 16, TOK), f32(SOURCES, 16, TOK),
+        bf16(SOURCES, HEADS, 144, TOK), bf16(SOURCES, 16, TOK), bf16(SOURCES, 16, TOK), bf16(SOURCES, 16, TOK),
         bf16(32, TOK), bf16(HEADS, 32, TOK), f32(2, 32, LENGTH), bf16(2, HEAD_DIM, LENGTH),
         f32(2, HEAD_DIM, LENGTH), f32(2, HEAD_DIM, LENGTH), bf16(HEADS, 32, TOK), bf16(HEADS, 32, TOK),
         bf16(PIECES, 32, 128), bf16(32, 32, 128), bf16(16, 32, 128), bf16(32, 32, 128),
@@ -567,7 +593,7 @@
         one, sems(ZCHUNKS), one, one, one, sems(ZCHUNKS),
         one, one, one, one, one, one, one, one,
         one, one, one, one, one, one,
-        one, one, one, one, one, one, one, one,
+        one, one, one, one, one, one, one, one, one,
     ]
 
 

time: 130 us -> 128 us (0.985)
  Pallas kernels: 129 us -> 127 us
    pallas_call x1, Pallas kernels: 127 us -> 125 us  [per_device(): pl.pallas_call(kernel, out_shape=(jax.ShapeDtypeStruct((TOK, D), BF16), j...]
where the time goes in v4:
time: 128 us; the launch traced here: 127 us
  Pallas kernels  127 us (99%)
    pallas_call x1, Pallas kernels, per_device(): pl.pallas_call(kernel, out_shape=(jax.ShapeDtypeStruct((TOK, D), BF16), j...  125 us

profile of v4, /device:TPU:1, one launch (start us, length us, event | category | flops | bytes accessed | tf_op | source)
XLA Modules:
  0.0 127.4 jit_solution(14468981201186774944)
XLA Ops:
  0.6 124.8 %shard_map.121 = (bf16[128,1152]{1,0:T(8,128)(2,1)}, bf16[64,1152]{1,0:T(8,128)(2,1)}, bf16[64,1152]{1,0:T(8,128)(2,1)}) custom-call(bf16[128,1152]{1,0:T(8,128)(2,1)} %bitcast.17, bf16[128,1152]{1,0:T(8,128)(2,1)} %bitcast.18, bf16[128,1152]{1,0:T(8,128)(2,1)} %bitcast.19, bf16[128,1152]{1,0:T(8,128)(2,1)} %bitcast.20, bf16[128,1152]{1,0:T(8,128)(2,1)} %bitcast.21, ...), custom_call_target="tpu_custom_call" | custom-call | tf_op jit(solution)/shard_map/pallas_call | solution.py:620
  125.4 2.0 %shard_map.122 = (bf16[128,1152]{1,0:T(8,128)(2,1)}, f32[64,1152]{1,0:T(8,128)}, f32[64,1152]{1,0:T(8,128)}) custom-call(bf16[128,1152]{1,0:T(8,128)(2,1)} %get-tuple-element.9.mixed, bf16[64,1152]{1,0:T(8,128)(2,1)} %get-tuple-element.10.ga, bf16[64,1152]{1,0:T(8,128)(2,1)} %get-tuple-element.11.gb), custom_call_target="tpu_custom_call" | custom-call | tf_op jit(solution)/shard_map/pallas_call | solution.py:634

commit v5 on v4

--- a/solution.py
+++ b/solution.py
@@ -18,7 +18,7 @@
 LENGTH = 1024
 CHUNK = 1024
 SOURCES = 4
-ZCHUNKS = 8
+ZCHUNKS = 4
 ZHEADS = HEADS // ZCHUNKS
 PIECES = 18
 SCALE = HEAD_DIM ** -0.5

time: 128 us -> 126 us (0.984)
  Pallas kernels: 127 us -> 125 us
    pallas_call x1, Pallas kernels: 125 us -> 123 us  [per_device(): pl.pallas_call(kernel, out_shape=(jax.ShapeDtypeStruct((TOK, D), BF16), j...]
where the time goes in v5:
time: 126 us
  Pallas kernels  125 us (99%)
    pallas_call x1, Pallas kernels, per_device(): pl.pallas_call(kernel, out_shape=(jax.ShapeDtypeStruct((TOK, D), BF16), j...  123 us

profile of v5, /device:TPU:1, one launch (start us, length us, event | category | flops | bytes accessed | tf_op | source)
XLA Modules:
  0.0 125.9 jit_solution(3184265216936646113)
XLA Ops:
  0.6 123.3 %shard_map.121 = (bf16[128,1152]{1,0:T(8,128)(2,1)}, bf16[64,1152]{1,0:T(8,128)(2,1)}, bf16[64,1152]{1,0:T(8,128)(2,1)}) custom-call(bf16[128,1152]{1,0:T(8,128)(2,1)} %bitcast.17, bf16[128,1152]{1,0:T(8,128)(2,1)} %bitcast.18, bf16[128,1152]{1,0:T(8,128)(2,1)} %bitcast.19, bf16[128,1152]{1,0:T(8,128)(2,1)} %bitcast.20, bf16[128,1152]{1,0:T(8,128)(2,1)} %bitcast.21, ...), custom_call_target="tpu_custom_call" | custom-call | tf_op jit(solution)/shard_map/pallas_call | solution.py:620
  123.9 2.0 %shard_map.122 = (bf16[128,1152]{1,0:T(8,128)(2,1)}, f32[64,1152]{1,0:T(8,128)}, f32[64,1152]{1,0:T(8,128)}) custom-call(bf16[128,1152]{1,0:T(8,128)(2,1)} %get-tuple-element.9.mixed, bf16[64,1152]{1,0:T(8,128)(2,1)} %get-tuple-element.10.ga, bf16[64,1152]{1,0:T(8,128)(2,1)} %get-tuple-element.11.gb), custom_call_target="tpu_custom_call" | custom-call | tf_op jit(solution)/shard_map/pallas_call | solution.py:634
